TPU v7x, 256 devices: a whole 4x4x8 slice. The times are simulated.
256 devices in a mesh: src: 16 (over x, y_lo, core), rcv: 16 (over z, y_hi).
Axes of the slice: x: 4, y: 4 (y_hi: 2, y_lo: 2; y = y_hi * 2 + y_lo), z: 8, core: 2. Of those that a mesh axis runs over, the one named last changes fastest.
Arguments:
- records: float32 [2048, 20480], P(('rcv', 'src')), may hold values from -500 to 500
- starts: int32 [2], replicated, may hold values from 0 to 10180, as said below
- block_mask: int32 [16, 16, 16], P('rcv', None, 'src'), may hold values from 0 to 1, as said below
Outputs:
- stacked: bfloat16 [2048, 16, 16, 8, 128], P('rcv', None, 'src')
Inputs may be any that keep to these rules, and one draw needn't show every extreme that they name: Some window starts at 10180. block_mask[a, b, c] is 0 wherever b < a.
All inputs are finite; a program needn't handle non-finite values.
Results may differ from a plain program's by a relative error of at most 0.0065.
Values may be sent and summed in bfloat16 or wider, within the bound.
No kernel may reach another device: no remote copies, remote signals or barrier semaphores. Data moves between devices by JAX's collectives and lax.ppermute only.
A program may use at most 192 MiB of HBM per device.

v0:
```python
import math

import jax
import jax.numpy as jnp
from jax import lax
from jax.sharding import PartitionSpec as P

DEC = 5
KSEG = 13
NT = 2048
FB = 512
HALF = 64
LAGS = 128
TAPS = 65
F = 1024
RAW = 10300


eps_power = 1e-06


def from_behind(block, axis, distance):
    devices = range(lax.axis_size(axis))
    route = [((i - distance) % len(devices), i) for i in devices]
    return lax.ppermute(block, axis, route)


def lowpass():
    tap_index = jnp.arange(TAPS, dtype=jnp.float32)
    centre = (TAPS - 1) / 2.0
    taper = 0.5 - 0.5 * jnp.cos(2.0 * math.pi * (tap_index + 1.0) / (TAPS + 1.0))
    return jnp.sinc((tap_index - centre) / DEC) * taper / DEC


def decimate(windows):
    taps_kernel = lowpass()
    frames = windows.reshape(windows.shape[0], windows.shape[1], NT + KSEG - 1, DEC)
    traces = jnp.zeros((windows.shape[0], windows.shape[1], NT), jnp.float32)
    for segment in range(KSEG):
        weights = taps_kernel[segment * DEC : (segment + 1) * DEC]
        traces = traces + jnp.sum(frames[:, :, segment : segment + NT, :] * weights, axis=3)
    return traces


def smoother(bins, band, reach):
    source_bins = jnp.arange(bins, dtype=jnp.int32)[:, None]
    target_bins = jnp.arange(band, dtype=jnp.int32)[None, :]
    inside = jnp.abs(source_bins - target_bins) <= reach
    lowest = jnp.maximum(target_bins - reach, 0)
    highest = jnp.minimum(target_bins + reach, bins - 1)
    counted = (highest - lowest + 1).astype(jnp.float32)
    return jnp.where(inside, 1.0, 0.0).astype(jnp.float32) / counted


def fourier_table(samples, bins):
    sample_ids = jnp.arange(samples, dtype=jnp.int32)[:, None]
    bin_ids = jnp.arange(bins, dtype=jnp.int32)[None, :]
    phase_index = sample_ids * bin_ids % samples
    radians = 2.0 * math.pi / samples * phase_index.astype(jnp.float32)
    return jnp.concatenate([jnp.cos(radians), -jnp.sin(radians)], axis=1)


def whiten(records, starts):
    windows = jax.vmap(
        lambda window_start: lax.dynamic_slice_in_dim(records, window_start, RAW, 1)
    )(starts)
    traces = decimate(windows)
    used_bins = FB + HALF
    spectrum = jnp.dot(
        traces.reshape(-1, NT), fourier_table(NT, used_bins), precision=lax.Precision.HIGHEST
    )
    real_part = spectrum[:, :used_bins]
    imag_part = spectrum[:, used_bins:]
    power = real_part * real_part + imag_part * imag_part
    weights = smoother(F, FB, HALF)[:used_bins]
    smoothed = jnp.dot(power, weights, precision=lax.Precision.HIGHEST)
    divisor = jnp.sqrt(smoothed + eps_power)
    whitened = jnp.stack([real_part[:, :FB] / divisor, imag_part[:, :FB] / divisor], axis=1)
    whitened = whitened.reshape(traces.shape[0], traces.shape[1], 2, FB)
    return jnp.transpose(whitened, (1, 0, 2, 3)).astype(jnp.bfloat16)


def lag_table(band, lag_count, samples):
    bin_ids = jnp.arange(band, dtype=jnp.int32)[:, None]
    lag_ids = jnp.arange(lag_count, dtype=jnp.int32)[None, :] - lag_count // 2 + samples
    phase_index = bin_ids * lag_ids % samples
    radians = 2.0 * math.pi / samples * phase_index.astype(jnp.float32)
    return jnp.concatenate([jnp.cos(radians), -jnp.sin(radians)], axis=0).astype(jnp.bfloat16)


def correlate(sources, receivers, inverse):
    rotated = jnp.stack([-receivers[:, :, 1], receivers[:, :, 0]], axis=2)
    paired = jnp.stack([receivers, rotated], axis=1)
    cross = jnp.einsum("iwpf,jqwpf->ijqf", sources, paired, preferred_element_type=jnp.float32)
    cross = cross.astype(jnp.bfloat16)
    cross = cross.reshape(-1, 2 * cross.shape[3])
    return jnp.dot(cross, inverse, preferred_element_type=jnp.float32)


def on_device(records, starts, block_mask):
    own_spec = whiten(records, starts)
    piece_rows = own_spec.shape[0]
    sources = lax.all_gather(own_spec, "src", axis=0, tiled=True)
    block_rows = sources.shape[0]
    axis_count = lax.axis_size("rcv")
    inverse = lag_table(FB, LAGS, NT)
    normalizer = 1.0 / math.sqrt(own_spec.shape[1] * own_spec.shape[3])
    block_row = block_mask.reshape(-1)
    src_index = lax.axis_index("src")
    rcv_index = lax.axis_index("rcv")
    source_ids = rcv_index * block_rows + jnp.arange(block_rows, dtype=jnp.int32)
    pieces_all = jnp.arange(axis_count, dtype=jnp.int32)

    def evaluate(receivers, first_row):
        count_rows = receivers.shape[0]
        gathered = first_row + jnp.arange(count_rows, dtype=jnp.int32)
        position = gathered // piece_rows
        receiver_ids = position * block_rows + src_index * piece_rows + gathered % piece_rows
        allowed = jnp.sum(
            jnp.where(position[:, None] == pieces_all[None, :], block_row[None, :], 0), axis=1
        )
        lagged = (
            correlate(sources, receivers, inverse).reshape(block_rows, count_rows, LAGS)
            * normalizer
        )
        keep_pair = (source_ids[:, None] < receiver_ids[None, :]) & (allowed[None, :] > 0)
        return jnp.where(keep_pair[:, :, None], lagged, 0.0).astype(jnp.bfloat16)

    def place(result, receivers, position):
        wanted = jnp.sum(jnp.where(pieces_all == position, block_row, 0))

        def compute(held):
            return evaluate(held, position * piece_rows)

        def nothing(held):
            return jnp.zeros((block_rows, held.shape[0], LAGS), jnp.bfloat16)

        values = lax.cond(wanted > 0, compute, nothing, receivers)
        return lax.dynamic_update_slice(result, values[:, None], (0, position, 0, 0))

    result = jnp.zeros((block_rows, axis_count, piece_rows, LAGS), jnp.bfloat16)
    result = place(result, own_spec, rcv_index)

    def advance(turn_index, loop_state):
        holding, current = loop_state
        holding = from_behind(holding, "rcv", 1)
        return (holding, place(current, holding, (rcv_index - turn_index) % axis_count))

    _, result = lax.fori_loop(1, axis_count, advance, (own_spec, result))
    return result.reshape(block_rows, axis_count, 1, piece_rows, LAGS)


def solution(mesh):
    in_specs = (P(("rcv", "src"), None), P(), P("rcv", None, "src"))
    out_specs = P("rcv", None, "src", None, None)
    return jax.shard_map(
        on_device, mesh=mesh, in_specs=in_specs, out_specs=out_specs, check_vma=False
    )
```

profile of v0, /device:TPU:8, one launch (start us, length us, event | category | flops | bytes accessed | tf_op | source)
XLA Modules:
  0.0 374.8 jit_solution(2086830780552123803)
XLA Ops:
  1.0 5.0 %while.20 = (s32[]{:T(128)}, f32[8,20480]{1,0:T(8,128)}, s32[2,2]{1,0:T(2,128)S(1)}, f32[2,8,10300]{2,1,0:T(8,128)S(1)}, s32[]{:T(128)}) while((s32[]{:T(128)}, f32[8,20480]{1,0:T(8,128)}, s32[2,2]{1,0:T(2,128)S(1)}, f32[2,8,10300]{2,1,0:T(8,128)S(1)}, s32[]{:T(128)}) %tuple.119), condition=%wide.while_cond, body=%wide.while_body.sunk | while | flops 2 | bytes 661473 | solution.py:65
  6.0 15.9 %reshape.278 = f32[2,8,2060,5]{3,2,1,0:T(8,128)} reshape(f32[2,8,10300]{2,1,0:T(8,128)S(1)} %get-tuple-element.344) | data formatting | bytes 1318400 | tf_op jit(solution)/shard_map/reshape | solution.py:37
  21.9 56.5 %fusion.29 = (f32[2,8,2048]{2,1,0:T(8,128)S(1)}, f32[2,8,2048]{2,1,0:T(8,128)S(1)}, f32[2,8,2048]{2,1,0:T(8,128)S(1)}, f32[2,8,2048]{2,1,0:T(8,128)S(1)}, f32[2,...) fusion(f32[2,8,2060,5]{3,2,1,0:T(8,128)} %reshape.278, ...), kind=kLoop, calls=%fused_computation.74 | loop fusion | flops 2654208 | bytes 7078068 | tf_op jit(solution)/shard_map/reduce_sum | solution.py:41
  78.4 26.0 %fusion.30 = (f32[2,8,2048]{2,1,0:T(8,128)S(1)}, f32[2,8,2048]{2,1,0:T(8,128)S(1)}, f32[2,8,2048]{2,1,0:T(8,128)S(1)}, f32[2,8,2048]{2,1,0:T(8,128)S(1)}) fusion(f32[2,8,2060,5]{3,2,1,0:T(8,128)} %reshape.278, f32[5]{0:T(128)S(1)} %get-tuple-element.520, f32[5]{0:T(128)S(1)} %get-tuple-element.517, f32[5]{0:T(128)S(1)} %get-tuple-element.518, ...), kind=kLoop, calls=%fused_computation.76 | loop fusion | flops 1179648 | bytes 3145808 | tf_op jit(solution)/shard_map/reduce_sum | solution.py:41
  104.4 20.8 %sine_negate_fusion = (f32[2048,576]{1,0:T(8,128)S(1)}, f32[2048,576]{1,0:T(8,128)S(1)}) fusion(), kind=kLoop, calls=%fused_computation.87 | loop fusion | flops 17694720 | bytes 9437184 | tf_op jit(solution)/shard_map/neg | solution.py:60
  125.2 5.5 %fusion.31 = f32[16,1152]{1,0:T(8,128)S(1)} fusion(f32[2048,576]{1,0:T(8,128)S(1)} %get-tuple-element.521, f32[2048,576]{1,0:T(8,128)S(1)} %get-tuple-element.522, f32[2,8,2048]{2,1,0:T(8,128)S(1)} %get-tuple-element.454, f32[2,8,2048]{2,1,0:T(8,128)S(1)} %get-tuple-element.455, f32[2,8,2048]{2,1,0:T(8,128)S(1)} %get-tuple-element.456, ...), kind=kOutput, calls=%fused_computation.77 | convolution fusion | flops 455737344 | bytes 11214848 | tf_op jit(solution)/shard_map/dot_general | solution.py:69
  131.6 19.6 %all_gather.3 = bf16[128,2,2,512]{3,2,1,0:T(2,128)(2,1)S(1)} all-gather(bf16[8,2,2,512]{3,2,1,0:T(2,128)(2,1)S(1)} %maximum_bitcast_fusion.2), channel_id=1, replica_groups=mesh['src'=16,'rcv'=16] {'src'}, dimensions={0}, use_global_device_ids=true | all-gather | bytes 557056 | tf_op jit(solution)/shard_map/all_gather | solution.py:103
  154.5 6.5 %conditional.2 = (bf16[128,1,8,128]{3,0,2,1:T(8,128)(2,1)S(1)}) conditional(s32[]{:T(128)} %convert_element_type.62, () %tuple.43, (s32[]{:T(128)}, s32[]{:T(128)}, s32[]{:T(128)}, s32[16]{0:T(128)S(1)}, s32[1,16,1]{1,2,0:T(1,128)S(1)}, /*index=5*/bf16[8,2,2,512]{3,2,1,0:T(2,128)(2,1)S(1)}, bf16[128,2,2,512]{3,2,1,0:T(2,128)(2,1)S(1)}, ...), branch_computations={%region_14.15_spmd, %region_15.17_spmd} | conditional | flops 278325952 | bytes 11014012 | solution.py:138
  156.3 2.1 fusion.4
  161.0 3.0 broadcast_in_dim.130
  165.8 201.9 %while.21 = (s32[]{:T(128)}, bf16[8,2,2,512]{3,0,2,1:T(8,128)(2,1)S(1)}, bf16[128,16,8,128]{3,0,2,1:T(8,128)(2,1)}, s32[]{:T(128)}, s32[16]{0:T(128)S(1)}, /*ind...) while((s32[]{:T(128)}, ...), condition=%wide.region_22.23_spmd.clone.clone, body=%wide.region_17.22_spmd.clone.clone.sunk | while | flops 278326016 | bytes 10621862 | solution.py:149
  167.3 6.7 %collective-permute-done = bf16[8,2,2,512]{3,0,2,1:T(8,128)(2,1)S(1)} collective-permute-done((bf16[8,2,2,512]{3,0,2,1:T(8,128)(2,1)S(1)}, bf16[8,2,2,512]{3,0,2,1:T(8,128)(2,1)S(1)}, u32[]{:S(2)}, u32[]{:S(2)}) %collective-permute-start) | collective-permute-done | bytes 32800 | tf_op jit(solution)/shard_map/while/body/eval_jaxpr/ppermute | solution.py:25
  174.0 5.5 %conditional.6 = (bf16[128,1,8,128]{3,0,2,1:T(8,128)(2,1)S(1)}) conditional(s32[]{:T(128)} %convert_element_type.94, () %tuple.117, (s32[]{:T(128)}, s32[]{:T(128)}, s32[]{:T(128)}, s32[16]{0:T(128)S(1)}, s32[1,16,1]{1,2,0:T(1,128)S(1)}, /*index=5*/bf16[8,2,2,512]{3,0,2,1:T(8,128)(2,1)S(1)}, bf16[128,2,2,512]{0,1,2,3:T(2,128)(2,1)S(1)}, ...), branch_computations={%region_19.19_spmd, %region_20.21_spmd} | conditional | flops 278325952 | bytes 9899900 | solution.py:138
  174.8 2.1 fusion.10
  181.6 6.1 %collective-permute-done = bf16[8,2,2,512]{3,0,2,1:T(8,128)(2,1)S(1)} collective-permute-done((bf16[8,2,2,512]{3,0,2,1:T(8,128)(2,1)S(1)}, bf16[8,2,2,512]{3,0,2,1:T(8,128)(2,1)S(1)}, u32[]{:S(2)}, u32[]{:S(2)}) %collective-permute-start) | collective-permute-done | bytes 32800 | tf_op jit(solution)/shard_map/while/body/eval_jaxpr/ppermute | solution.py:25
  187.8 5.5 %conditional.6 = (bf16[128,1,8,128]{3,0,2,1:T(8,128)(2,1)S(1)}) conditional(s32[]{:T(128)} %convert_element_type.94, () %tuple.117, (s32[]{:T(128)}, s32[]{:T(128)}, s32[]{:T(128)}, s32[16]{0:T(128)S(1)}, s32[1,16,1]{1,2,0:T(1,128)S(1)}, /*index=5*/bf16[8,2,2,512]{3,0,2,1:T(8,128)(2,1)S(1)}, bf16[128,2,2,512]{0,1,2,3:T(2,128)(2,1)S(1)}, ...), branch_computations={%region_19.19_spmd, %region_20.21_spmd} | conditional | flops 278325952 | bytes 9899900 | solution.py:138
  188.6 2.1 fusion.10
  195.4 6.1 %collective-permute-done = bf16[8,2,2,512]{3,0,2,1:T(8,128)(2,1)S(1)} collective-permute-done((bf16[8,2,2,512]{3,0,2,1:T(8,128)(2,1)S(1)}, bf16[8,2,2,512]{3,0,2,1:T(8,128)(2,1)S(1)}, u32[]{:S(2)}, u32[]{:S(2)}) %collective-permute-start) | collective-permute-done | bytes 32800 | tf_op jit(solution)/shard_map/while/body/eval_jaxpr/ppermute | solution.py:25
  201.6 5.5 %conditional.6 = (bf16[128,1,8,128]{3,0,2,1:T(8,128)(2,1)S(1)}) conditional(s32[]{:T(128)} %convert_element_type.94, () %tuple.117, (s32[]{:T(128)}, s32[]{:T(128)}, s32[]{:T(128)}, s32[16]{0:T(128)S(1)}, s32[1,16,1]{1,2,0:T(1,128)S(1)}, /*index=5*/bf16[8,2,2,512]{3,0,2,1:T(8,128)(2,1)S(1)}, bf16[128,2,2,512]{0,1,2,3:T(2,128)(2,1)S(1)}, ...), branch_computations={%region_19.19_spmd, %region_20.21_spmd} | conditional | flops 278325952 | bytes 9899900 | solution.py:138
  202.4 2.1 fusion.10
  209.2 6.1 %collective-permute-done = bf16[8,2,2,512]{3,0,2,1:T(8,128)(2,1)S(1)} collective-permute-done((bf16[8,2,2,512]{3,0,2,1:T(8,128)(2,1)S(1)}, bf16[8,2,2,512]{3,0,2,1:T(8,128)(2,1)S(1)}, u32[]{:S(2)}, u32[]{:S(2)}) %collective-permute-start) | collective-permute-done | bytes 32800 | tf_op jit(solution)/shard_map/while/body/eval_jaxpr/ppermute | solution.py:25
  215.3 5.5 %conditional.6 = (bf16[128,1,8,128]{3,0,2,1:T(8,128)(2,1)S(1)}) conditional(s32[]{:T(128)} %convert_element_type.94, () %tuple.117, (s32[]{:T(128)}, s32[]{:T(128)}, s32[]{:T(128)}, s32[16]{0:T(128)S(1)}, s32[1,16,1]{1,2,0:T(1,128)S(1)}, /*index=5*/bf16[8,2,2,512]{3,0,2,1:T(8,128)(2,1)S(1)}, bf16[128,2,2,512]{0,1,2,3:T(2,128)(2,1)S(1)}, ...), branch_computations={%region_19.19_spmd, %region_20.21_spmd} | conditional | flops 278325952 | bytes 9899900 | solution.py:138
  216.1 2.1 fusion.10
  223.0 6.1 %collective-permute-done = bf16[8,2,2,512]{3,0,2,1:T(8,128)(2,1)S(1)} collective-permute-done((bf16[8,2,2,512]{3,0,2,1:T(8,128)(2,1)S(1)}, bf16[8,2,2,512]{3,0,2,1:T(8,128)(2,1)S(1)}, u32[]{:S(2)}, u32[]{:S(2)}) %collective-permute-start) | collective-permute-done | bytes 32800 | tf_op jit(solution)/shard_map/while/body/eval_jaxpr/ppermute | solution.py:25
  229.1 5.5 %conditional.6 = (bf16[128,1,8,128]{3,0,2,1:T(8,128)(2,1)S(1)}) conditional(s32[]{:T(128)} %convert_element_type.94, () %tuple.117, (s32[]{:T(128)}, s32[]{:T(128)}, s32[]{:T(128)}, s32[16]{0:T(128)S(1)}, s32[1,16,1]{1,2,0:T(1,128)S(1)}, /*index=5*/bf16[8,2,2,512]{3,0,2,1:T(8,128)(2,1)S(1)}, bf16[128,2,2,512]{0,1,2,3:T(2,128)(2,1)S(1)}, ...), branch_computations={%region_19.19_spmd, %region_20.21_spmd} | conditional | flops 278325952 | bytes 9899900 | solution.py:138
  236.8 6.1 %collective-permute-done = bf16[8,2,2,512]{3,0,2,1:T(8,128)(2,1)S(1)} collective-permute-done((bf16[8,2,2,512]{3,0,2,1:T(8,128)(2,1)S(1)}, bf16[8,2,2,512]{3,0,2,1:T(8,128)(2,1)S(1)}, u32[]{:S(2)}, u32[]{:S(2)}) %collective-permute-start) | collective-permute-done | bytes 32800 | tf_op jit(solution)/shard_map/while/body/eval_jaxpr/ppermute | solution.py:25
  242.9 5.5 %conditional.6 = (bf16[128,1,8,128]{3,0,2,1:T(8,128)(2,1)S(1)}) conditional(s32[]{:T(128)} %convert_element_type.94, () %tuple.117, (s32[]{:T(128)}, s32[]{:T(128)}, s32[]{:T(128)}, s32[16]{0:T(128)S(1)}, s32[1,16,1]{1,2,0:T(1,128)S(1)}, /*index=5*/bf16[8,2,2,512]{3,0,2,1:T(8,128)(2,1)S(1)}, bf16[128,2,2,512]{0,1,2,3:T(2,128)(2,1)S(1)}, ...), branch_computations={%region_19.19_spmd, %region_20.21_spmd} | conditional | flops 278325952 | bytes 9899900 | solution.py:138
  243.7 2.1 fusion.10
  250.5 6.1 %collective-permute-done = bf16[8,2,2,512]{3,0,2,1:T(8,128)(2,1)S(1)} collective-permute-done((bf16[8,2,2,512]{3,0,2,1:T(8,128)(2,1)S(1)}, bf16[8,2,2,512]{3,0,2,1:T(8,128)(2,1)S(1)}, u32[]{:S(2)}, u32[]{:S(2)}) %collective-permute-start) | collective-permute-done | bytes 32800 | tf_op jit(solution)/shard_map/while/body/eval_jaxpr/ppermute | solution.py:25
  256.7 5.5 %conditional.6 = (bf16[128,1,8,128]{3,0,2,1:T(8,128)(2,1)S(1)}) conditional(s32[]{:T(128)} %convert_element_type.94, () %tuple.117, (s32[]{:T(128)}, s32[]{:T(128)}, s32[]{:T(128)}, s32[16]{0:T(128)S(1)}, s32[1,16,1]{1,2,0:T(1,128)S(1)}, /*index=5*/bf16[8,2,2,512]{3,0,2,1:T(8,128)(2,1)S(1)}, bf16[128,2,2,512]{0,1,2,3:T(2,128)(2,1)S(1)}, ...), branch_computations={%region_19.19_spmd, %region_20.21_spmd} | conditional | flops 278325952 | bytes 9899900 | solution.py:138
  257.5 2.1 fusion.10
  264.3 6.1 %collective-permute-done = bf16[8,2,2,512]{3,0,2,1:T(8,128)(2,1)S(1)} collective-permute-done((bf16[8,2,2,512]{3,0,2,1:T(8,128)(2,1)S(1)}, bf16[8,2,2,512]{3,0,2,1:T(8,128)(2,1)S(1)}, u32[]{:S(2)}, u32[]{:S(2)}) %collective-permute-start) | collective-permute-done | bytes 32800 | tf_op jit(solution)/shard_map/while/body/eval_jaxpr/ppermute | solution.py:25
  270.4 5.5 %conditional.6 = (bf16[128,1,8,128]{3,0,2,1:T(8,128)(2,1)S(1)}) conditional(s32[]{:T(128)} %convert_element_type.94, () %tuple.117, (s32[]{:T(128)}, s32[]{:T(128)}, s32[]{:T(128)}, s32[16]{0:T(128)S(1)}, s32[1,16,1]{1,2,0:T(1,128)S(1)}, /*index=5*/bf16[8,2,2,512]{3,0,2,1:T(8,128)(2,1)S(1)}, bf16[128,2,2,512]{0,1,2,3:T(2,128)(2,1)S(1)}, ...), branch_computations={%region_19.19_spmd, %region_20.21_spmd} | conditional | flops 278325952 | bytes 9899900 | solution.py:138
  278.1 6.1 %collective-permute-done = bf16[8,2,2,512]{3,0,2,1:T(8,128)(2,1)S(1)} collective-permute-done((bf16[8,2,2,512]{3,0,2,1:T(8,128)(2,1)S(1)}, bf16[8,2,2,512]{3,0,2,1:T(8,128)(2,1)S(1)}, u32[]{:S(2)}, u32[]{:S(2)}) %collective-permute-start) | collective-permute-done | bytes 32800 | tf_op jit(solution)/shard_map/while/body/eval_jaxpr/ppermute | solution.py:25
  285.0 3.4 collective-permute-start
  289.8 2.8 collective-permute-done
  292.6 5.5 %conditional.6 = (bf16[128,1,8,128]{3,0,2,1:T(8,128)(2,1)S(1)}) conditional(s32[]{:T(128)} %convert_element_type.94, () %tuple.117, (s32[]{:T(128)}, s32[]{:T(128)}, s32[]{:T(128)}, s32[16]{0:T(128)S(1)}, s32[1,16,1]{1,2,0:T(1,128)S(1)}, /*index=5*/bf16[8,2,2,512]{3,0,2,1:T(8,128)(2,1)S(1)}, bf16[128,2,2,512]{0,1,2,3:T(2,128)(2,1)S(1)}, ...), branch_computations={%region_19.19_spmd, %region_20.21_spmd} | conditional | flops 278325952 | bytes 9899900 | solution.py:138
  301.5 4.9 %collective-permute-done = bf16[8,2,2,512]{3,0,2,1:T(8,128)(2,1)S(1)} collective-permute-done((bf16[8,2,2,512]{3,0,2,1:T(8,128)(2,1)S(1)}, bf16[8,2,2,512]{3,0,2,1:T(8,128)(2,1)S(1)}, u32[]{:S(2)}, u32[]{:S(2)}) %collective-permute-start) | collective-permute-done | bytes 32800 | tf_op jit(solution)/shard_map/while/body/eval_jaxpr/ppermute | solution.py:25
  306.3 5.5 %conditional.6 = (bf16[128,1,8,128]{3,0,2,1:T(8,128)(2,1)S(1)}) conditional(s32[]{:T(128)} %convert_element_type.94, () %tuple.117, (s32[]{:T(128)}, s32[]{:T(128)}, s32[]{:T(128)}, s32[16]{0:T(128)S(1)}, s32[1,16,1]{1,2,0:T(1,128)S(1)}, /*index=5*/bf16[8,2,2,512]{3,0,2,1:T(8,128)(2,1)S(1)}, bf16[128,2,2,512]{0,1,2,3:T(2,128)(2,1)S(1)}, ...), branch_computations={%region_19.19_spmd, %region_20.21_spmd} | conditional | flops 278325952 | bytes 9899900 | solution.py:138
  314.0 6.1 %collective-permute-done = bf16[8,2,2,512]{3,0,2,1:T(8,128)(2,1)S(1)} collective-permute-done((bf16[8,2,2,512]{3,0,2,1:T(8,128)(2,1)S(1)}, bf16[8,2,2,512]{3,0,2,1:T(8,128)(2,1)S(1)}, u32[]{:S(2)}, u32[]{:S(2)}) %collective-permute-start) | collective-permute-done | bytes 32800 | tf_op jit(solution)/shard_map/while/body/eval_jaxpr/ppermute | solution.py:25
  320.1 5.5 %conditional.6 = (bf16[128,1,8,128]{3,0,2,1:T(8,128)(2,1)S(1)}) conditional(s32[]{:T(128)} %convert_element_type.94, () %tuple.117, (s32[]{:T(128)}, s32[]{:T(128)}, s32[]{:T(128)}, s32[16]{0:T(128)S(1)}, s32[1,16,1]{1,2,0:T(1,128)S(1)}, /*index=5*/bf16[8,2,2,512]{3,0,2,1:T(8,128)(2,1)S(1)}, bf16[128,2,2,512]{0,1,2,3:T(2,128)(2,1)S(1)}, ...), branch_computations={%region_19.19_spmd, %region_20.21_spmd} | conditional | flops 278325952 | bytes 9899900 | solution.py:138
  327.8 6.1 %collective-permute-done = bf16[8,2,2,512]{3,0,2,1:T(8,128)(2,1)S(1)} collective-permute-done((bf16[8,2,2,512]{3,0,2,1:T(8,128)(2,1)S(1)}, bf16[8,2,2,512]{3,0,2,1:T(8,128)(2,1)S(1)}, u32[]{:S(2)}, u32[]{:S(2)}) %collective-permute-start) | collective-permute-done | bytes 32800 | tf_op jit(solution)/shard_map/while/body/eval_jaxpr/ppermute | solution.py:25
  333.9 5.5 %conditional.6 = (bf16[128,1,8,128]{3,0,2,1:T(8,128)(2,1)S(1)}) conditional(s32[]{:T(128)} %convert_element_type.94, () %tuple.117, (s32[]{:T(128)}, s32[]{:T(128)}, s32[]{:T(128)}, s32[16]{0:T(128)S(1)}, s32[1,16,1]{1,2,0:T(1,128)S(1)}, /*index=5*/bf16[8,2,2,512]{3,0,2,1:T(8,128)(2,1)S(1)}, bf16[128,2,2,512]{0,1,2,3:T(2,128)(2,1)S(1)}, ...), branch_computations={%region_19.19_spmd, %region_20.21_spmd} | conditional | flops 278325952 | bytes 9899900 | solution.py:138
  341.5 6.1 %collective-permute-done = bf16[8,2,2,512]{3,0,2,1:T(8,128)(2,1)S(1)} collective-permute-done((bf16[8,2,2,512]{3,0,2,1:T(8,128)(2,1)S(1)}, bf16[8,2,2,512]{3,0,2,1:T(8,128)(2,1)S(1)}, u32[]{:S(2)}, u32[]{:S(2)}) %collective-permute-start) | collective-permute-done | bytes 32800 | tf_op jit(solution)/shard_map/while/body/eval_jaxpr/ppermute | solution.py:25
  347.7 5.5 %conditional.6 = (bf16[128,1,8,128]{3,0,2,1:T(8,128)(2,1)S(1)}) conditional(s32[]{:T(128)} %convert_element_type.94, () %tuple.117, (s32[]{:T(128)}, s32[]{:T(128)}, s32[]{:T(128)}, s32[16]{0:T(128)S(1)}, s32[1,16,1]{1,2,0:T(1,128)S(1)}, /*index=5*/bf16[8,2,2,512]{3,0,2,1:T(8,128)(2,1)S(1)}, bf16[128,2,2,512]{0,1,2,3:T(2,128)(2,1)S(1)}, ...), branch_computations={%region_19.19_spmd, %region_20.21_spmd} | conditional | flops 278325952 | bytes 9899900 | solution.py:138
  355.3 6.1 %collective-permute-done = bf16[8,2,2,512]{3,0,2,1:T(8,128)(2,1)S(1)} collective-permute-done((bf16[8,2,2,512]{3,0,2,1:T(8,128)(2,1)S(1)}, bf16[8,2,2,512]{3,0,2,1:T(8,128)(2,1)S(1)}, u32[]{:S(2)}, u32[]{:S(2)}) %collective-permute-start) | collective-permute-done | bytes 32800 | tf_op jit(solution)/shard_map/while/body/eval_jaxpr/ppermute | solution.py:25
  361.5 5.5 %conditional.6 = (bf16[128,1,8,128]{3,0,2,1:T(8,128)(2,1)S(1)}) conditional(s32[]{:T(128)} %convert_element_type.94, () %tuple.117, (s32[]{:T(128)}, s32[]{:T(128)}, s32[]{:T(128)}, s32[16]{0:T(128)S(1)}, s32[1,16,1]{1,2,0:T(1,128)S(1)}, /*index=5*/bf16[8,2,2,512]{3,0,2,1:T(8,128)(2,1)S(1)}, bf16[128,2,2,512]{0,1,2,3:T(2,128)(2,1)S(1)}, ...), branch_computations={%region_19.19_spmd, %region_20.21_spmd} | conditional | flops 278325952 | bytes 9899900 | solution.py:138
  367.7 6.9 %copy.58 = bf16[128,16,8,128]{3,2,1,0:T(8,128)(2,1)} copy(bf16[128,16,8,128]{3,0,2,1:T(8,128)(2,1)} %get-tuple-element.336) | data formatting | bytes 8388608 | tf_op jit(solution)/shard_map/while | solution.py:149
  (294 shorter events, 101.9 us)
Async XLA Ops:
  130.7 22.3 %copy-start = (s32[1,16,1]{1,2,0:T(1,128)S(1)}, s32[1,16,1]{1,2,0:T(1,128)}, u32[]{:S(2)}) copy-start(s32[1,16,1]{1,2,0:T(1,128)} %param.11) | copy-start | bytes 196
  165.8 8.2 %collective-permute-start = (bf16[8,2,2,512]{3,0,2,1:T(8,128)(2,1)S(1)}, bf16[8,2,2,512]{3,0,2,1:T(8,128)(2,1)S(1)}, u32[]{:S(2)}, u32[]{:S(2)}) collective-permute-start(bf16[8,2,2,512]{3,0,2,1:T(8,128)(2,1)S(1)} %get-tuple-element.639), channel_id=1, source_target_pairs={{15,0},{0,1},{1,2},{2,3},{3,4},{4,5},{5,6},{6,7},{7,8},{8,9},{9,10... | collective-permute-start | bytes 98312 | tf_op jit(solution)/shard_map/while/body/eval_jaxpr/ppermute | solution.py:25
  180.3 7.5 %collective-permute-start = (bf16[8,2,2,512]{3,0,2,1:T(8,128)(2,1)S(1)}, bf16[8,2,2,512]{3,0,2,1:T(8,128)(2,1)S(1)}, u32[]{:S(2)}, u32[]{:S(2)}) collective-permute-start(bf16[8,2,2,512]{3,0,2,1:T(8,128)(2,1)S(1)} %get-tuple-element.639), channel_id=1, source_target_pairs={{15,0},{0,1},{1,2},{2,3},{3,4},{4,5},{5,6},{6,7},{7,8},{8,9},{9,10... | collective-permute-start | bytes 98312 | tf_op jit(solution)/shard_map/while/body/eval_jaxpr/ppermute | solution.py:25
  194.0 7.5 %collective-permute-start = (bf16[8,2,2,512]{3,0,2,1:T(8,128)(2,1)S(1)}, bf16[8,2,2,512]{3,0,2,1:T(8,128)(2,1)S(1)}, u32[]{:S(2)}, u32[]{:S(2)}) collective-permute-start(bf16[8,2,2,512]{3,0,2,1:T(8,128)(2,1)S(1)} %get-tuple-element.639), channel_id=1, source_target_pairs={{15,0},{0,1},{1,2},{2,3},{3,4},{4,5},{5,6},{6,7},{7,8},{8,9},{9,10... | collective-permute-start | bytes 98312 | tf_op jit(solution)/shard_map/while/body/eval_jaxpr/ppermute | solution.py:25
  207.8 7.5 %collective-permute-start = (bf16[8,2,2,512]{3,0,2,1:T(8,128)(2,1)S(1)}, bf16[8,2,2,512]{3,0,2,1:T(8,128)(2,1)S(1)}, u32[]{:S(2)}, u32[]{:S(2)}) collective-permute-start(bf16[8,2,2,512]{3,0,2,1:T(8,128)(2,1)S(1)} %get-tuple-element.639), channel_id=1, source_target_pairs={{15,0},{0,1},{1,2},{2,3},{3,4},{4,5},{5,6},{6,7},{7,8},{8,9},{9,10... | collective-permute-start | bytes 98312 | tf_op jit(solution)/shard_map/while/body/eval_jaxpr/ppermute | solution.py:25
  221.6 7.5 %collective-permute-start = (bf16[8,2,2,512]{3,0,2,1:T(8,128)(2,1)S(1)}, bf16[8,2,2,512]{3,0,2,1:T(8,128)(2,1)S(1)}, u32[]{:S(2)}, u32[]{:S(2)}) collective-permute-start(bf16[8,2,2,512]{3,0,2,1:T(8,128)(2,1)S(1)} %get-tuple-element.639), channel_id=1, source_target_pairs={{15,0},{0,1},{1,2},{2,3},{3,4},{4,5},{5,6},{6,7},{7,8},{8,9},{9,10... | collective-permute-start | bytes 98312 | tf_op jit(solution)/shard_map/while/body/eval_jaxpr/ppermute | solution.py:25
  235.4 7.5 %collective-permute-start = (bf16[8,2,2,512]{3,0,2,1:T(8,128)(2,1)S(1)}, bf16[8,2,2,512]{3,0,2,1:T(8,128)(2,1)S(1)}, u32[]{:S(2)}, u32[]{:S(2)}) collective-permute-start(bf16[8,2,2,512]{3,0,2,1:T(8,128)(2,1)S(1)} %get-tuple-element.639), channel_id=1, source_target_pairs={{15,0},{0,1},{1,2},{2,3},{3,4},{4,5},{5,6},{6,7},{7,8},{8,9},{9,10... | collective-permute-start | bytes 98312 | tf_op jit(solution)/shard_map/while/body/eval_jaxpr/ppermute | solution.py:25
  249.1 7.5 %collective-permute-start = (bf16[8,2,2,512]{3,0,2,1:T(8,128)(2,1)S(1)}, bf16[8,2,2,512]{3,0,2,1:T(8,128)(2,1)S(1)}, u32[]{:S(2)}, u32[]{:S(2)}) collective-permute-start(bf16[8,2,2,512]{3,0,2,1:T(8,128)(2,1)S(1)} %get-tuple-element.639), channel_id=1, source_target_pairs={{15,0},{0,1},{1,2},{2,3},{3,4},{4,5},{5,6},{6,7},{7,8},{8,9},{9,10... | collective-permute-start | bytes 98312 | tf_op jit(solution)/shard_map/while/body/eval_jaxpr/ppermute | solution.py:25
  262.9 7.5 %collective-permute-start = (bf16[8,2,2,512]{3,0,2,1:T(8,128)(2,1)S(1)}, bf16[8,2,2,512]{3,0,2,1:T(8,128)(2,1)S(1)}, u32[]{:S(2)}, u32[]{:S(2)}) collective-permute-start(bf16[8,2,2,512]{3,0,2,1:T(8,128)(2,1)S(1)} %get-tuple-element.639), channel_id=1, source_target_pairs={{15,0},{0,1},{1,2},{2,3},{3,4},{4,5},{5,6},{6,7},{7,8},{8,9},{9,10... | collective-permute-start | bytes 98312 | tf_op jit(solution)/shard_map/while/body/eval_jaxpr/ppermute | solution.py:25
  276.7 7.5 %collective-permute-start = (bf16[8,2,2,512]{3,0,2,1:T(8,128)(2,1)S(1)}, bf16[8,2,2,512]{3,0,2,1:T(8,128)(2,1)S(1)}, u32[]{:S(2)}, u32[]{:S(2)}) collective-permute-start(bf16[8,2,2,512]{3,0,2,1:T(8,128)(2,1)S(1)} %get-tuple-element.639), channel_id=1, source_target_pairs={{15,0},{0,1},{1,2},{2,3},{3,4},{4,5},{5,6},{6,7},{7,8},{8,9},{9,10... | collective-permute-start | bytes 98312 | tf_op jit(solution)/shard_map/while/body/eval_jaxpr/ppermute | solution.py:25
  285.0 7.5 %collective-permute-start = (bf16[8,2,2,512]{3,0,2,1:T(8,128)(2,1)S(1)}, bf16[8,2,2,512]{3,0,2,1:T(8,128)(2,1)S(1)}, u32[]{:S(2)}, u32[]{:S(2)}) collective-permute-start(bf16[8,2,2,512]{3,0,2,1:T(8,128)(2,1)S(1)} %get-tuple-element.639), channel_id=1, source_target_pairs={{15,0},{0,1},{1,2},{2,3},{3,4},{4,5},{5,6},{6,7},{7,8},{8,9},{9,10... | collective-permute-start | bytes 98312 | tf_op jit(solution)/shard_map/while/body/eval_jaxpr/ppermute | solution.py:25
  298.8 7.5 %collective-permute-start = (bf16[8,2,2,512]{3,0,2,1:T(8,128)(2,1)S(1)}, bf16[8,2,2,512]{3,0,2,1:T(8,128)(2,1)S(1)}, u32[]{:S(2)}, u32[]{:S(2)}) collective-permute-start(bf16[8,2,2,512]{3,0,2,1:T(8,128)(2,1)S(1)} %get-tuple-element.639), channel_id=1, source_target_pairs={{15,0},{0,1},{1,2},{2,3},{3,4},{4,5},{5,6},{6,7},{7,8},{8,9},{9,10... | collective-permute-start | bytes 98312 | tf_op jit(solution)/shard_map/while/body/eval_jaxpr/ppermute | solution.py:25
  312.6 7.5 %collective-permute-start = (bf16[8,2,2,512]{3,0,2,1:T(8,128)(2,1)S(1)}, bf16[8,2,2,512]{3,0,2,1:T(8,128)(2,1)S(1)}, u32[]{:S(2)}, u32[]{:S(2)}) collective-permute-start(bf16[8,2,2,512]{3,0,2,1:T(8,128)(2,1)S(1)} %get-tuple-element.639), channel_id=1, source_target_pairs={{15,0},{0,1},{1,2},{2,3},{3,4},{4,5},{5,6},{6,7},{7,8},{8,9},{9,10... | collective-permute-start | bytes 98312 | tf_op jit(solution)/shard_map/while/body/eval_jaxpr/ppermute | solution.py:25
  326.4 7.5 %collective-permute-start = (bf16[8,2,2,512]{3,0,2,1:T(8,128)(2,1)S(1)}, bf16[8,2,2,512]{3,0,2,1:T(8,128)(2,1)S(1)}, u32[]{:S(2)}, u32[]{:S(2)}) collective-permute-start(bf16[8,2,2,512]{3,0,2,1:T(8,128)(2,1)S(1)} %get-tuple-element.639), channel_id=1, source_target_pairs={{15,0},{0,1},{1,2},{2,3},{3,4},{4,5},{5,6},{6,7},{7,8},{8,9},{9,10... | collective-permute-start | bytes 98312 | tf_op jit(solution)/shard_map/while/body/eval_jaxpr/ppermute | solution.py:25
  340.2 7.5 %collective-permute-start = (bf16[8,2,2,512]{3,0,2,1:T(8,128)(2,1)S(1)}, bf16[8,2,2,512]{3,0,2,1:T(8,128)(2,1)S(1)}, u32[]{:S(2)}, u32[]{:S(2)}) collective-permute-start(bf16[8,2,2,512]{3,0,2,1:T(8,128)(2,1)S(1)} %get-tuple-element.639), channel_id=1, source_target_pairs={{15,0},{0,1},{1,2},{2,3},{3,4},{4,5},{5,6},{6,7},{7,8},{8,9},{9,10... | collective-permute-start | bytes 98312 | tf_op jit(solution)/shard_map/while/body/eval_jaxpr/ppermute | solution.py:25
  353.9 7.5 %collective-permute-start = (bf16[8,2,2,512]{3,0,2,1:T(8,128)(2,1)S(1)}, bf16[8,2,2,512]{3,0,2,1:T(8,128)(2,1)S(1)}, u32[]{:S(2)}, u32[]{:S(2)}) collective-permute-start(bf16[8,2,2,512]{3,0,2,1:T(8,128)(2,1)S(1)} %get-tuple-element.639), channel_id=1, source_target_pairs={{15,0},{0,1},{1,2},{2,3},{3,4},{4,5},{5,6},{6,7},{7,8},{8,9},{9,10... | collective-permute-start | bytes 98312 | tf_op jit(solution)/shard_map/while/body/eval_jaxpr/ppermute | solution.py:25
where the time goes:
time: 382 us; the launch traced here: 375 us
  other arithmetic  122 us (32%)
  waiting for transfers between devices  88 us (23%)
  local copies, waits for them, and re-layouts  64.6 us (17%)
  matrix products  63.7 us (17%)
  blocking collectives  19.6 us (5%)
  loops' own time  11.5 us (3%)
  starting transfers between devices  4.74 us (1%)
    ppermute x15, waiting for transfers between devices, from_behind(): return lax.ppermute(block, axis, route)  88 us
    reduce_sum x2, other arithmetic, decimate(): jnp.sum(frames[:, :, segment:segment + NT, :] * weights, axis=3)  82.5 us
    dot_general x15, matrix products, correlate(): jnp.einsum('iwpf,jqwpf->ijqf', sources, paired, preferred_element_type=jn...  31.7 us
    dot_general x15, matrix products, correlate(): return jnp.dot(cross, inverse, preferred_element_type=jnp.float32)  25.7 us
    neg x1, other arithmetic, fourier_table(): return jnp.concatenate([jnp.cos(radians), -jnp.sin(radians)], axis=1)  20.8 us
    all_gather x1, blocking collectives, on_device(): sources = lax.all_gather(own_spec, 'src', axis=0, tiled=True)  19.6 us
    reshape x1, local copies, waits for them, and re-layouts, decimate(): windows.reshape(windows.shape[0], windows.shape[1], NT + KSEG - 1, DEC)  15.9 us
    dynamic_update_slice x16, local copies, waits for them, and re-layouts, place(): lax.dynamic_update_slice(result, values[:, None], (0, position, 0, 0))  11.7 us
  transfers between devices with their start and end apart: 15, of which 15 were waited for; matrix products, arithmetic and copies ran while one was open for 3% of the time, Pallas kernels for 0%

commit v1 on v0

v1 whole, which is shorter than its diff:
```python
import functools
import math

import jax
import jax.numpy as jnp
import numpy as np
from jax import lax
from jax.experimental import pallas as pl
from jax.experimental.pallas import tpu as pltpu
from jax.sharding import PartitionSpec as P

DEC = 5
NT = 2048
FB = 512
HALF = 64
LAGS = 128
TAPS = 65
F = 1024
RAW = 10300
WINDOWS = 2
BLOCKS = 16
PIECE = 8
GROUP = 16
LANES = 128
FINE = 8
COARSE = LAGS // FINE
EPS = 1e-06
SPEC = WINDOWS * 2 * FB


def lowpass():
    k = np.arange(TAPS, dtype=np.float64)
    taper = 0.5 - 0.5 * np.cos(2.0 * np.pi * (k + 1.0) / (TAPS + 1.0))
    return np.sinc((k - (TAPS - 1) / 2.0) / DEC) * taper / DEC


def decimation_matrix():
    taps = lowpass()
    matrix = np.zeros((6 * LANES, LANES))
    for n in range(LANES):
        matrix[DEC * n : DEC * n + TAPS, n] = taps
    return matrix.astype(np.float32)


def tile_bins():
    bins = -np.ones((8, LANES), np.int64)
    first = np.zeros((8, LANES), np.int64)
    for tile in range(8):
        pair, side = tile // 2, tile % 2
        for half in range(2):
            low = (0, 8)[half] if tile == 0 else (tile, GROUP - tile)[half]
            for high in range((FB + HALF) // GROUP):
                if high < FB // GROUP:
                    column = side * 64 + half * 32 + high
                else:
                    column = (1 - side) * 64 + pair * 8 + half * 4 + high - FB // GROUP
                bins[tile, column] = GROUP * high + low
                first[tile, column] = half
    return bins, first


def fourier_tiles():
    bins, half_of = tile_bins()
    m = np.arange(LANES)
    tiles = np.zeros((8, 2 * LANES, 2 * LANES))
    for tile in range(8):
        for column in range(LANES):
            f = bins[tile, column]
            if f < 0:
                continue
            angle = 2.0 * np.pi * ((f * m) % NT) / NT
            c, s = np.cos(angle), np.sin(angle)
            half = half_of[tile, column]
            if tile == 0:
                rows = slice(half * LANES, (half + 1) * LANES)
                tiles[tile, rows, column] = c
                tiles[tile, rows, LANES + column] = -s
            else:
                sign = 1.0 if half == 0 else -1.0
                tiles[tile, :LANES, column] = c
                tiles[tile, LANES:, column] = sign * s
                tiles[tile, :LANES, LANES + column] = -s
                tiles[tile, LANES:, LANES + column] = sign * c
    return tiles.astype(np.float32)


def band_bins():
    bins, _ = tile_bins()
    band = []
    extra = -np.ones(LANES, np.int64)
    for pair in range(4):
        left, right = bins[2 * pair], bins[2 * pair + 1]
        band.append(np.where(np.arange(LANES) < 64, left, right))
        swapped = np.where(np.arange(LANES) < 64, right, left)
        extra = np.where(swapped >= 0, swapped, extra)
    return np.concatenate(band), extra


def smoother():
    band, extra = band_bins()
    source = np.concatenate([band, extra])[:, None]
    target = band[None, :]
    inside = (np.abs(source - target) <= HALF) & (source >= 0)
    counted = np.minimum(band + HALF, F - 1) - np.maximum(band - HALF, 0) + 1
    return inside.astype(np.float32), (1.0 / counted).astype(np.float32)[None, :]


def phases(lags, scale):
    band, _ = band_bins()
    angle = 2.0 * np.pi * ((lags[:, None] * band[None, :]) % NT) / NT
    return np.stack([np.cos(angle), np.sin(angle)]).astype(np.float32) * np.float32(scale)


def plus(a, b):
    if a is None:
        return b
    return a if b is None else a + b


def minus(a, b):
    if b is None:
        return a
    return -b if a is None else a - b


def times(a, factor):
    return None if a is None or factor == 0.0 else (a if factor == 1.0 else (-a if factor == -1.0 else a * factor))


def small_fourier(values):
    count = len(values)
    if count == 1:
        return values
    even, odd = small_fourier(values[0::2]), small_fourier(values[1::2])
    low, high = [], []
    for f in range(count // 2):
        angle = 2.0 * math.pi * f / count
        c, s = math.cos(angle), math.sin(angle)
        c = 0.0 if 4 * f == count else c
        real, imag = odd[f]
        turned = (plus(times(real, c), times(imag, s)), minus(times(imag, c), times(real, s)))
        low.append((plus(even[f][0], turned[0]), plus(even[f][1], turned[1])))
        high.append((minus(even[f][0], turned[0]), minus(even[f][1], turned[1])))
    return low + high


def whiten_kernel(starts, records, decimate, fourier, smooth, inverse_count, out, raw):
    lane = lax.broadcasted_iota(jnp.int32, (PIECE, LANES), 1)
    used = 5 * GROUP + 1
    last_tile = records.shape[1] // LANES - 1
    for w in range(WINDOWS):
        start = starts[w]
        base = start // LANES
        offset = start % LANES
        turn = (LANES - offset) % LANES
        own = lane < LANES - offset

        def turned(v):
            at = jnp.minimum(base + v, last_tile)
            return pltpu.roll(records[:, pl.ds(pl.multiple_of(at * LANES, LANES), LANES)], turn, 1)

        now = turned(0)
        for v in range(used):
            later = turned(v + 1)
            moved = jnp.where(own, now, later)
            now = later
            run, part = v // 5, v % 5
            if run < GROUP:
                raw[run * 16 + w * 8 : run * 16 + w * 8 + 8, part * LANES : (part + 1) * LANES] = moved
            if part == 0 and run > 0:
                raw[(run - 1) * 16 + w * 8 : (run - 1) * 16 + w * 8 + 8, 5 * LANES :] = moved
    traces = jnp.dot(raw[...], decimate[...], precision=lax.Precision.HIGHEST, preferred_element_type=jnp.float32)
    parts = small_fourier([(traces[16 * run : 16 * run + 16], None) for run in range(GROUP)])
    left = lax.broadcasted_iota(jnp.int32, (16, LANES), 1) < 64
    real_tiles, imag_tiles = [], []
    for tile in range(8):
        if tile == 0:
            pair = [parts[0][0], parts[8][0]]
        else:
            pair = list(parts[tile])
        both = jnp.dot(
            jnp.concatenate(pair, axis=1), fourier[tile], precision=lax.Precision.HIGHEST,
            preferred_element_type=jnp.float32,
        )
        real_tiles.append(both[:, :LANES])
        imag_tiles.append(both[:, LANES:])
    reals, imags, powers = [], [], []
    extra = None
    for pair in range(4):
        ra, rb = real_tiles[2 * pair], real_tiles[2 * pair + 1]
        ia, ib = imag_tiles[2 * pair], imag_tiles[2 * pair + 1]
        reals.append(jnp.where(left, ra, rb))
        imags.append(jnp.where(left, ia, ib))
        pa, pb = ra * ra + ia * ia, rb * rb + ib * ib
        powers.append(jnp.where(left, pa, pb))
        extra = plus(extra, jnp.where(left, pb, pa))
    power = jnp.concatenate(powers + [extra], axis=1)
    first = power.astype(jnp.bfloat16)
    rest = power - first.astype(jnp.float32)
    second = rest.astype(jnp.bfloat16)
    third = (rest - second.astype(jnp.float32)).astype(jnp.bfloat16)
    sums = jnp.dot(
        jnp.concatenate([first, second, third], axis=0), smooth[...], preferred_element_type=jnp.float32
    )
    smoothed = (sums[:16] + sums[16:32] + sums[32:]) * inverse_count[...]
    gain = lax.rsqrt(smoothed + EPS)
    for q, values in enumerate((reals, imags)):
        white = (jnp.concatenate(values, axis=1) * gain).astype(jnp.bfloat16)
        for w in range(WINDOWS):
            out[:, (2 * w + q) * FB : (2 * w + q + 1) * FB] = white[8 * w : 8 * w + 8]


def whiten(records, starts):
    decimate = decimation_matrix()
    fourier = fourier_tiles()
    smooth, inverse_count = smoother()
    vmem = pl.BlockSpec(memory_space=pltpu.VMEM)
    return pl.pallas_call(
        whiten_kernel,
        out_shape=jax.ShapeDtypeStruct((PIECE, SPEC), jnp.bfloat16),
        in_specs=[pl.BlockSpec(memory_space=pltpu.SMEM)] + [vmem] * 5,
        out_specs=vmem,
        scratch_shapes=[pltpu.VMEM((16 * GROUP, 6 * LANES), jnp.float32)],
        compiler_params=pltpu.CompilerParams(vmem_limit_bytes=32 * 1024 * 1024),
    )(
        starts, records, jnp.asarray(decimate), jnp.asarray(fourier),
        jnp.asarray(smooth).astype(jnp.bfloat16), jnp.asarray(inverse_count),
    )


def swap_groups(values):
    lane_group = lax.broadcasted_iota(jnp.int32, values[0].shape, 1) // FINE
    values = list(values)
    for bit in (3, 2, 1, 0):
        distance = 1 << bit
        low_half = (lane_group & distance) == 0
        for a in range(COARSE):
            if a & distance:
                continue
            low, high = values[a], values[a + distance]
            shift = distance * FINE
            values[a] = jnp.where(low_half, low, pltpu.roll(high, shift, 1))
            values[a + distance] = jnp.where(low_half, pltpu.roll(low, LANES - shift, 1), high)
    return values


def correlate_kernel(places, limits, order, mine, other, receivers, fine, coarse, out, turned, spread, sources):
    step = pl.program_id(0)

    @pl.when(step == 0)
    def _():
        for side, rows in enumerate((mine, other)):

            @pl.loop(0, 8)
            def _(piece):
                at = pl.multiple_of(places[side * 8 + piece] * PIECE, PIECE)
                values = rows[piece].astype(jnp.float32)
                sources[...] = values
                for pair in range(PIECE // 2):
                    for w in range(WINDOWS):
                        at_w = 2 * w * FB
                        reals, imags = [], []
                        for k in range(2):
                            ch = 2 * pair + k
                            real = jnp.broadcast_to(sources[ch : ch + 1, at_w : at_w + FB], (FINE, FB))
                            imag = jnp.broadcast_to(sources[ch : ch + 1, at_w + FB : at_w + 2 * FB], (FINE, FB))
                            c, s = fine[0], fine[1]
                            reals.append(real * c - imag * s)
                            imags.append(real * s + imag * c)
                        target = pl.ds(pl.multiple_of(at * FINE + pair * 16, 16), 16)
                        turned[target, at_w : at_w + FB] = jnp.concatenate(reals, 0).astype(jnp.bfloat16)
                        turned[target, at_w + FB : at_w + 2 * FB] = jnp.concatenate(imags, 0).astype(jnp.bfloat16)

    for piece in range(2):
        held = receivers[0, piece].astype(jnp.float32)
        for w in range(WINDOWS):
            at_w = 2 * w * FB
            real, imag = held[:, at_w : at_w + FB], held[:, at_w + FB : at_w + 2 * FB]
            for pair in range(COARSE // 2):
                reals, imags = [], []
                for k in range(2):
                    lag = 2 * pair + k
                    c = jnp.broadcast_to(coarse[0, lag : lag + 1], (PIECE, FB))
                    s = jnp.broadcast_to(coarse[1, lag : lag + 1], (PIECE, FB))
                    reals.append(real * c - imag * s)
                    imags.append(real * s + imag * c)
                row = piece * COARSE * PIECE + pair * 16
                spread[row : row + 16, at_w : at_w + FB] = jnp.concatenate(reals, 0).astype(jnp.bfloat16)
                spread[row : row + 16, at_w + FB : at_w + 2 * FB] = jnp.concatenate(imags, 0).astype(jnp.bfloat16)

    sublane = lax.broadcasted_iota(jnp.int32, (PIECE, LANES), 0)
    for chunk in range(4):
        lagged = lax.dot_general(
            spread[...], turned[chunk * 256 : (chunk + 1) * 256, :], (((1,), (1,)), ((), ())),
            preferred_element_type=jnp.float32,
        )
        for piece in range(2):
            limit = sublane + limits[2 * order[step] + piece]
            for half in range(2):
                rows = piece * COARSE * PIECE
                values = [
                    lagged[rows + lag * PIECE : rows + (lag + 1) * PIECE, half * LANES : (half + 1) * LANES]
                    for lag in range(COARSE)
                ]
                for k, value in enumerate(swap_groups(values)):
                    source = chunk * 32 + half * 16 + k
                    out[source, piece] = jnp.where(limit > source, value, 0.0).astype(jnp.bfloat16)


def correlate(places, limits, order, mine, other, receivers):
    fine = phases(np.arange(FINE), 1.0)
    coarse = phases(-(FINE * np.arange(COARSE) - LAGS // 2), 1.0 / math.sqrt(WINDOWS * FB))
    whole = lambda *shape: pl.BlockSpec(shape, lambda i, *_: (0,) * len(shape))
    grid_spec = pltpu.PrefetchScalarGridSpec(
        num_scalar_prefetch=3,
        grid=(8,),
        in_specs=[
            whole(8, PIECE, SPEC), whole(8, PIECE, SPEC),
            pl.BlockSpec((1, 2, PIECE, SPEC), lambda i, *_: (i, 0, 0, 0)),
            whole(2, FINE, FB), whole(2, COARSE, FB),
        ],
        out_specs=pl.BlockSpec((128, 2, PIECE, LAGS), lambda i, places, limits, order: (0, order[i], 0, 0)),
        scratch_shapes=[
            pltpu.VMEM((128 * FINE, SPEC), jnp.bfloat16),
            pltpu.VMEM((2 * COARSE * PIECE, SPEC), jnp.bfloat16),
            pltpu.VMEM((PIECE, SPEC), jnp.float32),
        ],
    )
    return pl.pallas_call(
        correlate_kernel,
        grid_spec=grid_spec,
        out_shape=jax.ShapeDtypeStruct((128, BLOCKS, PIECE, LAGS), jnp.bfloat16),
        compiler_params=pltpu.CompilerParams(vmem_limit_bytes=40 * 1024 * 1024),
    )(places, limits, order, mine, other, receivers, jnp.asarray(fine), jnp.asarray(coarse))


def move(block, axis, source_of):
    return lax.ppermute(block, axis, [(source_of(i), i) for i in range(lax.axis_size(axis))])


def on_device(records, starts, block_mask):
    own = whiten(records, starts)
    src = lax.axis_index("src")
    rcv = lax.axis_index("rcv")
    x, y_lo, core = src // 4, (src // 2) % 2, src % 2
    z, y_hi = rcv // 2, rcv % 2

    near = move(own, "src", lambda i: i ^ 2)
    two = jnp.where(y_lo == 0, jnp.stack([own, near]), jnp.stack([near, own]))
    mine = [two] + [
        move(two, "src", lambda i, k=k: ((i // 4 + k) % 4) * 4 + i % 4) for k in (1, 2, 3)
    ]
    mine = jnp.concatenate(mine, axis=0)
    other = move(mine, "src", lambda i: i ^ 1)

    far = move(own, "rcv", lambda i: i ^ 1)
    pair = jnp.where(y_hi == 0, jnp.stack([own, far]), jnp.stack([far, own]))
    pairs = [pair] + [
        move(pair, "rcv", lambda i, k=k: ((i // 2 + k) % 8) * 2 + i % 2) for k in range(1, 8)
    ]
    receivers = jnp.stack(pairs)

    k = jnp.arange(8, dtype=jnp.int32)
    chip = ((x + k // 2) % 4) * 4 + (k % 2) * 2
    places = jnp.concatenate([chip + core, chip + 1 - core])
    order = (z + k) % 8
    pieces = jnp.arange(BLOCKS, dtype=jnp.int32)
    wanted = block_mask.reshape(-1) > 0
    limits = jnp.where(
        wanted & (pieces >= rcv), jnp.where(pieces == rcv, src * PIECE, 4096), -4096
    ).astype(jnp.int32)
    result = correlate(places, limits, order, mine, other, receivers)
    return result.reshape(128, BLOCKS, 1, PIECE, LAGS)


def solution(mesh):
    in_specs = (P(("rcv", "src"), None), P(), P("rcv", None, "src"))
    out_specs = P("rcv", None, "src", None, None)
    return jax.shard_map(
        on_device, mesh=mesh, in_specs=in_specs, out_specs=out_specs, check_vma=False
    )
```

time: 382 us -> 71.5 us (0.19)
  the two profiles are of different devices: /device:TPU:8 before, /device:TPU:1 now
where the time goes in v1:
time: 71.5 us; the launch traced here: 70.9 us
  starting transfers between devices  35.9 us (50%)
  Pallas kernels  19.7 us (28%)
  waiting for transfers between devices  8.27 us (12%)
  local copies, waits for them, and re-layouts  6.15 us (9%)
  other arithmetic  0.82 us (1%)
    ppermute x13, starting transfers between devices, move(): lax.ppermute(block, axis, [(source_of(i), i) for i in range(lax.axis_size...  35.9 us
    pallas_call x1, Pallas kernels, correlate(): pl.pallas_call(correlate_kernel, grid_spec=grid_spec, out_shape=jax.Shape...  15.9 us
    ppermute x13, waiting for transfers between devices, move(): lax.ppermute(block, axis, [(source_of(i), i) for i in range(lax.axis_size...  8.27 us
    unnamed x22, local copies, waits for them, and re-layouts  6.14 us
    pallas_call x1, Pallas kernels, whiten(): pl.pallas_call(whiten_kernel, out_shape=jax.ShapeDtypeStruct((PIECE, SPEC...  3.79 us
  transfers between devices with their start and end apart: 13, of which 6 were waited for; matrix products, arithmetic and copies ran while one was open for 1% of the time, Pallas kernels for 0%

profile of v1, /device:TPU:1, one launch (start us, length us, event | category | flops | bytes accessed | tf_op | source)
XLA Modules:
  0.0 70.9 jit_solution(11985975759656843316)
XLA Ops:
  0.0 0.0 copy-start
  0.0 1.6 %copy-done = f32[8,256,256]{2,1,0:T(8,128)S(1)} copy-done((f32[8,256,256]{2,1,0:T(8,128)S(1)}, f32[8,256,256]{2,1,0:T(8,128)}, u32[]{:S(2)}) %copy-start) | copy-done | bytes 2097176
  1.6 0.0 copy-start.1
  1.6 1.1 %copy-done.1 = f32[8,20480]{1,0:T(8,128)S(1)} copy-done((f32[8,20480]{1,0:T(8,128)S(1)}, f32[8,20480]{1,0:T(8,128)}, u32[]{:S(2)}) %copy-start.1) | copy-done | bytes 655384
  2.7 0.0 copy-start.2
  2.7 1.1 %copy-done.2 = bf16[640,512]{1,0:T(8,128)(2,1)S(1)} copy-done((bf16[640,512]{1,0:T(8,128)(2,1)S(1)}, bf16[640,512]{1,0:T(8,128)(2,1)}, u32[]{:S(2)}) %copy-start.2) | copy-done | bytes 655384
  3.8 0.0 copy-start.3
  3.8 1.0 %copy-done.3 = f32[768,128]{1,0:T(8,128)S(1)} copy-done((f32[768,128]{1,0:T(8,128)S(1)}, f32[768,128]{1,0:T(8,128)}, u32[]{:S(2)}) %copy-start.3) | copy-done | bytes 393240
  4.8 0.0 copy-start.6
  4.8 0.7 copy-done.6
  5.4 0.0 copy-start.7
  5.4 0.7 copy-done.7
  6.1 0.0 copy-start.4
  6.1 0.0 copy-start.5
  6.1 3.8 %shard_map.91 = bf16[8,2048]{1,0:T(8,128)(2,1)S(1)} custom-call(s32[2]{0:T(128)S(1)} %copy-done.7, f32[8,20480]{1,0:T(8,128)S(1)} %copy-done.1, f32[768,128]{1,0:T(8,128)S(1)} %copy-done.3, f32[8,256,256]{2,1,0:T(8,128)S(1)} %copy-done, bf16[640,512]{1,0:T(8,128)(2,1)S(1)} %copy-done.2, f32[1,512]{1,0:T(1,128)S(1)} %copy-done.6), custom_call_target="tpu_custom_call" | custom-call | tf_op jit(solution)/shard_map/pallas_call | solution.py:218
  9.9 3.8 %collective-permute-start.5 = (bf16[8,2048]{1,0:T(8,128)(2,1)S(1)}, bf16[8,2048]{1,0:T(8,128)(2,1)S(1)}, u32[]{:S(2)}, u32[]{:S(2)}) collective-permute-start(bf16[8,2048]{1,0:T(8,128)(2,1)S(1)} %shard_map.91), channel_id=1, source_target_pairs={{1,0},{0,1},{3,2},{2,3},{5,4},{4,5},{7,6},{6,7},{9,8},{8,9},{11,10... | collective-permute-start | bytes 98312 | tf_op jit(solution)/shard_map/ppermute | solution.py:338
  13.7 0.4 collective-permute-start
  14.1 0.7 fusion.3.limits
  14.8 0.1 pad_add_fusion.places
  14.9 0.1 collective-permute-done.5
  15.0 1.7 %collective-permute-done = bf16[8,2048]{1,0:T(8,128)(2,1)S(1)} collective-permute-done((bf16[8,2048]{1,0:T(8,128)(2,1)S(1)}, bf16[8,2048]{1,0:T(8,128)(2,1)S(1)}, u32[]{:S(2)}, u32[]{:S(2)}) %collective-permute-start) | collective-permute-done | bytes 32800 | tf_op jit(solution)/shard_map/ppermute | solution.py:338
  16.8 1.3 %collective-permute-start.3 = (bf16[2,8,2048]{2,1,0:T(8,128)(2,1)S(1)}, bf16[2,8,2048]{2,1,0:T(8,128)(2,1)S(1)}, u32[]{:S(2)}, u32[]{:S(2)}) collective-permute-start(bf16[2,8,2048]{2,1,0:T(8,128)(2,1)S(1)} %get-tuple-element.6), channel_id=1, source_target_pairs={{192,0},{208,16},{224,32},{240,48},{0,64},{16,80},{32,96},{48,112}... | collective-permute-start | bytes 196616 | tf_op jit(solution)/shard_map/ppermute | solution.py:338
  18.1 2.4 %collective-permute-start.2 = (bf16[2,8,2048]{2,1,0:T(8,128)(2,1)S(1)}, bf16[2,8,2048]{2,1,0:T(8,128)(2,1)S(1)}, u32[]{:S(2)}, u32[]{:S(2)}) collective-permute-start(bf16[2,8,2048]{2,1,0:T(8,128)(2,1)S(1)} %get-tuple-element.6), channel_id=1, source_target_pairs={{128,0},{144,16},{160,32},{176,48},{192,64},{208,80},{224,96},{240... | collective-permute-start | bytes 196616 | tf_op jit(solution)/shard_map/ppermute | solution.py:338
  20.5 1.2 %collective-permute-start.1 = (bf16[2,8,2048]{2,1,0:T(8,128)(2,1)S(1)}, bf16[2,8,2048]{2,1,0:T(8,128)(2,1)S(1)}, u32[]{:S(2)}, u32[]{:S(2)}) collective-permute-start(bf16[2,8,2048]{2,1,0:T(8,128)(2,1)S(1)} %get-tuple-element.6), channel_id=1, source_target_pairs={{64,0},{80,16},{96,32},{112,48},{128,64},{144,80},{160,96},{176,11... | collective-permute-start | bytes 196616 | tf_op jit(solution)/shard_map/ppermute | solution.py:338
  21.7 1.6 %collective-permute-start.12 = (bf16[2,8,2048]{2,1,0:T(8,128)(2,1)S(1)}, bf16[2,8,2048]{2,1,0:T(8,128)(2,1)S(1)}, u32[]{:S(2)}, u32[]{:S(2)}) collective-permute-start(bf16[2,8,2048]{2,1,0:T(8,128)(2,1)S(1)} %get-tuple-element.5), channel_id=1, source_target_pairs={{14,0},{15,1},{0,2},{1,3},{2,4},{3,5},{4,6},{5,7},{6,8},{7,9},{8,1... | collective-permute-start | bytes 196616 | tf_op jit(solution)/shard_map/ppermute | solution.py:338
  23.3 3.9 %collective-permute-start.6 = (bf16[2,8,2048]{2,1,0:T(8,128)(2,1)S(1)}, bf16[2,8,2048]{2,1,0:T(8,128)(2,1)S(1)}, u32[]{:S(2)}, u32[]{:S(2)}) collective-permute-start(bf16[2,8,2048]{2,1,0:T(8,128)(2,1)S(1)} %get-tuple-element.5), channel_id=1, source_target_pairs={{2,0},{3,1},{4,2},{5,3},{6,4},{7,5},{8,6},{9,7},{10,8},{11,9},{12,... | collective-permute-start | bytes 196616 | tf_op jit(solution)/shard_map/ppermute | solution.py:338
  27.3 1.3 %collective-permute-done.6 = bf16[2,8,2048]{2,1,0:T(8,128)(2,1)S(1)} collective-permute-done((bf16[2,8,2048]{2,1,0:T(8,128)(2,1)S(1)}, bf16[2,8,2048]{2,1,0:T(8,128)(2,1)S(1)}, u32[]{:S(2)}, u32[]{:S(2)}) %collective-permute-start.6) | collective-permute-done | bytes 65568 | tf_op jit(solution)/shard_map/ppermute | solution.py:338
  28.6 3.0 %collective-permute-start.7 = (bf16[2,8,2048]{2,1,0:T(8,128)(2,1)S(1)}, bf16[2,8,2048]{2,1,0:T(8,128)(2,1)S(1)}, u32[]{:S(2)}, u32[]{:S(2)}) collective-permute-start(bf16[2,8,2048]{2,1,0:T(8,128)(2,1)S(1)} %get-tuple-element.5), channel_id=1, source_target_pairs={{4,0},{5,1},{6,2},{7,3},{8,4},{9,5},{10,6},{11,7},{12,8},{13,9},{1... | collective-permute-start | bytes 196616 | tf_op jit(solution)/shard_map/ppermute | solution.py:338
  31.6 1.3 %collective-permute-done.7 = bf16[2,8,2048]{2,1,0:T(8,128)(2,1)S(1)} collective-permute-done((bf16[2,8,2048]{2,1,0:T(8,128)(2,1)S(1)}, bf16[2,8,2048]{2,1,0:T(8,128)(2,1)S(1)}, u32[]{:S(2)}, u32[]{:S(2)}) %collective-permute-start.7) | collective-permute-done | bytes 65568 | tf_op jit(solution)/shard_map/ppermute | solution.py:338
  32.9 3.8 %collective-permute-start.11 = (bf16[2,8,2048]{2,1,0:T(8,128)(2,1)S(1)}, bf16[2,8,2048]{2,1,0:T(8,128)(2,1)S(1)}, u32[]{:S(2)}, u32[]{:S(2)}) collective-permute-start(bf16[2,8,2048]{2,1,0:T(8,128)(2,1)S(1)} %get-tuple-element.5), channel_id=1, source_target_pairs={{12,0},{13,1},{14,2},{15,3},{0,4},{1,5},{2,6},{3,7},{4,8},{5,9},{6... | collective-permute-start | bytes 196616 | tf_op jit(solution)/shard_map/ppermute | solution.py:338
  36.8 0.0 collective-permute-done.3
  36.8 1.8 %collective-permute-start.10 = (bf16[2,8,2048]{2,1,0:T(8,128)(2,1)S(1)}, bf16[2,8,2048]{2,1,0:T(8,128)(2,1)S(1)}, u32[]{:S(2)}, u32[]{:S(2)}) collective-permute-start(bf16[2,8,2048]{2,1,0:T(8,128)(2,1)S(1)} %get-tuple-element.5), channel_id=1, source_target_pairs={{10,0},{11,1},{12,2},{13,3},{14,4},{15,5},{0,6},{1,7},{2,8},{3,9},... | collective-permute-start | bytes 196616 | tf_op jit(solution)/shard_map/ppermute | solution.py:338
  38.5 0.0 collective-permute-done.2
  38.5 2.1 %collective-permute-start.9 = (bf16[2,8,2048]{2,1,0:T(8,128)(2,1)S(1)}, bf16[2,8,2048]{2,1,0:T(8,128)(2,1)S(1)}, u32[]{:S(2)}, u32[]{:S(2)}) collective-permute-start(bf16[2,8,2048]{2,1,0:T(8,128)(2,1)S(1)} %get-tuple-element.5), channel_id=1, source_target_pairs={{8,0},{9,1},{10,2},{11,3},{12,4},{13,5},{14,6},{15,7},{0,8},{1,9},... | collective-permute-start | bytes 196616 | tf_op jit(solution)/shard_map/ppermute | solution.py:338
  40.6 0.0 collective-permute-done.1
  40.6 2.8 %collective-permute-start.8 = (bf16[2,8,2048]{2,1,0:T(8,128)(2,1)S(1)}, bf16[2,8,2048]{2,1,0:T(8,128)(2,1)S(1)}, u32[]{:S(2)}, u32[]{:S(2)}) collective-permute-start(bf16[2,8,2048]{2,1,0:T(8,128)(2,1)S(1)} %get-tuple-element.5), channel_id=1, source_target_pairs={{6,0},{7,1},{8,2},{9,3},{10,4},{11,5},{12,6},{13,7},{14,8},{15,9},... | collective-permute-start | bytes 196616 | tf_op jit(solution)/shard_map/ppermute | solution.py:338
  43.5 2.7 %collective-permute-done.8 = bf16[2,8,2048]{2,1,0:T(8,128)(2,1)S(1)} collective-permute-done((bf16[2,8,2048]{2,1,0:T(8,128)(2,1)S(1)}, bf16[2,8,2048]{2,1,0:T(8,128)(2,1)S(1)}, u32[]{:S(2)}, u32[]{:S(2)}) %collective-permute-start.8) | collective-permute-done | bytes 65568 | tf_op jit(solution)/shard_map/ppermute | solution.py:338
  46.2 7.6 %collective-permute-start.4 = (bf16[8,8,2048]{2,1,0:T(8,128)(2,1)S(1)}, bf16[8,8,2048]{2,1,0:T(8,128)(2,1)S(1)}, u32[]{:S(2)}, u32[]{:S(2)}) collective-permute-start(bf16[8,8,2048]{2,1,0:T(8,128)(2,1)S(1)} %pad_maximum_fusion.mine), channel_id=1, source_target_pairs={{16,0},{0,16},{48,32},{32,48},{80,64},{64,80},{112,96},{96,112},{1... | collective-permute-start | bytes 786440 | tf_op jit(solution)/shard_map/ppermute | solution.py:338
  53.8 0.0 collective-permute-done.9
  53.9 0.0 collective-permute-done.10
  53.9 0.0 collective-permute-done.11
  53.9 0.0 collective-permute-done.12
  53.9 1.1 %collective-permute-done.4.other = bf16[8,8,2048]{2,1,0:T(8,128)(2,1)S(1)} collective-permute-done((bf16[8,8,2048]{2,1,0:T(8,128)(2,1)S(1)}, bf16[8,8,2048]{2,1,0:T(8,128)(2,1)S(1)}, u32[]{:S(2)}, u32[]{:S(2)}) %collective-permute-start.4) | collective-permute-done | bytes 262176 | tf_op jit(solution)/shard_map/ppermute | solution.py:338
  55.0 0.0 copy-done.4
  55.0 0.0 copy-done.5
  55.0 15.9 %shard_map.92 = bf16[128,16,8,128]{3,2,1,0:T(8,128)(2,1)} custom-call(s32[16]{0:T(128)S(1)} %pad_add_fusion.places, s32[16]{0:T(128)S(1)} %fusion.3.limits, s32[8]{0:T(128)S(1)} %and_select_fusion.order, bf16[8,8,2048]{2,1,0:T(8,128)(2,1)S(1)} %pad_maximum_fusion.mine, bf16[8,8,2048]{2,1,0:T(8,128)(2,1)S(1)} %collective-permute-done.4.other, ...), custom_call_target="tpu_custom_call" | custom-call | tf_op jit(solution)/shard_map/pallas_call | solution.py:329
  (12 shorter events, 0.1 us)
Async XLA Ops:
  0.0 1.6 %copy-start = (f32[8,256,256]{2,1,0:T(8,128)S(1)}, f32[8,256,256]{2,1,0:T(8,128)}, u32[]{:S(2)}) copy-start(f32[8,256,256]{2,1,0:T(8,128)} %constant.118.clone.fourier) | copy-start | bytes 6291460
  1.6 1.1 %copy-start.1 = (f32[8,20480]{1,0:T(8,128)S(1)}, f32[8,20480]{1,0:T(8,128)}, u32[]{:S(2)}) copy-start(f32[8,20480]{1,0:T(8,128)} %records.1) | copy-start | bytes 1966084
  2.7 1.1 %copy-start.2 = (bf16[640,512]{1,0:T(8,128)(2,1)S(1)}, bf16[640,512]{1,0:T(8,128)(2,1)}, u32[]{:S(2)}) copy-start(bf16[640,512]{1,0:T(8,128)(2,1)} %constant.125.smooth) | copy-start | bytes 1966084
  3.8 1.0 %copy-start.3 = (f32[768,128]{1,0:T(8,128)S(1)}, f32[768,128]{1,0:T(8,128)}, u32[]{:S(2)}) copy-start(f32[768,128]{1,0:T(8,128)} %constant.117.clone.decimate) | copy-start | bytes 1179652
  4.8 0.7 copy-start.6
  5.4 0.7 copy-start.7
  6.1 48.9 %copy-start.4 = (f32[2,16,512]{2,1,0:T(8,128)S(1)}, f32[2,16,512]{2,1,0:T(8,128)}, u32[]{:S(2)}) copy-start(f32[2,16,512]{2,1,0:T(8,128)} %constant.122.clone.coarse) | copy-start | bytes 196612
  6.1 48.9 %copy-start.5 = (f32[2,8,512]{2,1,0:T(8,128)S(1)}, f32[2,8,512]{2,1,0:T(8,128)}, u32[]{:S(2)}) copy-start(f32[2,8,512]{2,1,0:T(8,128)} %constant.121.clone.fine) | copy-start | bytes 98308
  9.9 5.1 %collective-permute-start.5 = (bf16[8,2048]{1,0:T(8,128)(2,1)S(1)}, bf16[8,2048]{1,0:T(8,128)(2,1)S(1)}, u32[]{:S(2)}, u32[]{:S(2)}) collective-permute-start(bf16[8,2048]{1,0:T(8,128)(2,1)S(1)} %shard_map.91), channel_id=1, source_target_pairs={{1,0},{0,1},{3,2},{2,3},{5,4},{4,5},{7,6},{6,7},{9,8},{8,9},{11,10... | collective-permute-start | bytes 98312 | tf_op jit(solution)/shard_map/ppermute | solution.py:338
  13.7 3.0 %collective-permute-start = (bf16[8,2048]{1,0:T(8,128)(2,1)S(1)}, bf16[8,2048]{1,0:T(8,128)(2,1)S(1)}, u32[]{:S(2)}, u32[]{:S(2)}) collective-permute-start(bf16[8,2048]{1,0:T(8,128)(2,1)S(1)} %shard_map.91), channel_id=1, source_target_pairs={{32,0},{48,16},{0,32},{16,48},{96,64},{112,80},{64,96},{80,112},{1... | collective-permute-start | bytes 98312 | tf_op jit(solution)/shard_map/ppermute | solution.py:338
  16.8 20.0 %collective-permute-start.3 = (bf16[2,8,2048]{2,1,0:T(8,128)(2,1)S(1)}, bf16[2,8,2048]{2,1,0:T(8,128)(2,1)S(1)}, u32[]{:S(2)}, u32[]{:S(2)}) collective-permute-start(bf16[2,8,2048]{2,1,0:T(8,128)(2,1)S(1)} %get-tuple-element.6), channel_id=1, source_target_pairs={{192,0},{208,16},{224,32},{240,48},{0,64},{16,80},{32,96},{48,112}... | collective-permute-start | bytes 196616 | tf_op jit(solution)/shard_map/ppermute | solution.py:338
  18.1 20.5 %collective-permute-start.2 = (bf16[2,8,2048]{2,1,0:T(8,128)(2,1)S(1)}, bf16[2,8,2048]{2,1,0:T(8,128)(2,1)S(1)}, u32[]{:S(2)}, u32[]{:S(2)}) collective-permute-start(bf16[2,8,2048]{2,1,0:T(8,128)(2,1)S(1)} %get-tuple-element.6), channel_id=1, source_target_pairs={{128,0},{144,16},{160,32},{176,48},{192,64},{208,80},{224,96},{240... | collective-permute-start | bytes 196616 | tf_op jit(solution)/shard_map/ppermute | solution.py:338
  20.5 20.1 %collective-permute-start.1 = (bf16[2,8,2048]{2,1,0:T(8,128)(2,1)S(1)}, bf16[2,8,2048]{2,1,0:T(8,128)(2,1)S(1)}, u32[]{:S(2)}, u32[]{:S(2)}) collective-permute-start(bf16[2,8,2048]{2,1,0:T(8,128)(2,1)S(1)} %get-tuple-element.6), channel_id=1, source_target_pairs={{64,0},{80,16},{96,32},{112,48},{128,64},{144,80},{160,96},{176,11... | collective-permute-start | bytes 196616 | tf_op jit(solution)/shard_map/ppermute | solution.py:338
  21.7 32.2 %collective-permute-start.12 = (bf16[2,8,2048]{2,1,0:T(8,128)(2,1)S(1)}, bf16[2,8,2048]{2,1,0:T(8,128)(2,1)S(1)}, u32[]{:S(2)}, u32[]{:S(2)}) collective-permute-start(bf16[2,8,2048]{2,1,0:T(8,128)(2,1)S(1)} %get-tuple-element.5), channel_id=1, source_target_pairs={{14,0},{15,1},{0,2},{1,3},{2,4},{3,5},{4,6},{5,7},{6,8},{7,9},{8,1... | collective-permute-start | bytes 196616 | tf_op jit(solution)/shard_map/ppermute | solution.py:338
  23.3 5.3 %collective-permute-start.6 = (bf16[2,8,2048]{2,1,0:T(8,128)(2,1)S(1)}, bf16[2,8,2048]{2,1,0:T(8,128)(2,1)S(1)}, u32[]{:S(2)}, u32[]{:S(2)}) collective-permute-start(bf16[2,8,2048]{2,1,0:T(8,128)(2,1)S(1)} %get-tuple-element.5), channel_id=1, source_target_pairs={{2,0},{3,1},{4,2},{5,3},{6,4},{7,5},{8,6},{9,7},{10,8},{11,9},{12,... | collective-permute-start | bytes 196616 | tf_op jit(solution)/shard_map/ppermute | solution.py:338
  28.6 4.3 %collective-permute-start.7 = (bf16[2,8,2048]{2,1,0:T(8,128)(2,1)S(1)}, bf16[2,8,2048]{2,1,0:T(8,128)(2,1)S(1)}, u32[]{:S(2)}, u32[]{:S(2)}) collective-permute-start(bf16[2,8,2048]{2,1,0:T(8,128)(2,1)S(1)} %get-tuple-element.5), channel_id=1, source_target_pairs={{4,0},{5,1},{6,2},{7,3},{8,4},{9,5},{10,6},{11,7},{12,8},{13,9},{1... | collective-permute-start | bytes 196616 | tf_op jit(solution)/shard_map/ppermute | solution.py:338
  32.9 21.0 %collective-permute-start.11 = (bf16[2,8,2048]{2,1,0:T(8,128)(2,1)S(1)}, bf16[2,8,2048]{2,1,0:T(8,128)(2,1)S(1)}, u32[]{:S(2)}, u32[]{:S(2)}) collective-permute-start(bf16[2,8,2048]{2,1,0:T(8,128)(2,1)S(1)} %get-tuple-element.5), channel_id=1, source_target_pairs={{12,0},{13,1},{14,2},{15,3},{0,4},{1,5},{2,6},{3,7},{4,8},{5,9},{6... | collective-permute-start | bytes 196616 | tf_op jit(solution)/shard_map/ppermute | solution.py:338
  36.8 17.1 %collective-permute-start.10 = (bf16[2,8,2048]{2,1,0:T(8,128)(2,1)S(1)}, bf16[2,8,2048]{2,1,0:T(8,128)(2,1)S(1)}, u32[]{:S(2)}, u32[]{:S(2)}) collective-permute-start(bf16[2,8,2048]{2,1,0:T(8,128)(2,1)S(1)} %get-tuple-element.5), channel_id=1, source_target_pairs={{10,0},{11,1},{12,2},{13,3},{14,4},{15,5},{0,6},{1,7},{2,8},{3,9},... | collective-permute-start | bytes 196616 | tf_op jit(solution)/shard_map/ppermute | solution.py:338
  38.5 15.3 %collective-permute-start.9 = (bf16[2,8,2048]{2,1,0:T(8,128)(2,1)S(1)}, bf16[2,8,2048]{2,1,0:T(8,128)(2,1)S(1)}, u32[]{:S(2)}, u32[]{:S(2)}) collective-permute-start(bf16[2,8,2048]{2,1,0:T(8,128)(2,1)S(1)} %get-tuple-element.5), channel_id=1, source_target_pairs={{8,0},{9,1},{10,2},{11,3},{12,4},{13,5},{14,6},{15,7},{0,8},{1,9},... | collective-permute-start | bytes 196616 | tf_op jit(solution)/shard_map/ppermute | solution.py:338
  40.6 5.6 %collective-permute-start.8 = (bf16[2,8,2048]{2,1,0:T(8,128)(2,1)S(1)}, bf16[2,8,2048]{2,1,0:T(8,128)(2,1)S(1)}, u32[]{:S(2)}, u32[]{:S(2)}) collective-permute-start(bf16[2,8,2048]{2,1,0:T(8,128)(2,1)S(1)} %get-tuple-element.5), channel_id=1, source_target_pairs={{6,0},{7,1},{8,2},{9,3},{10,4},{11,5},{12,6},{13,7},{14,8},{15,9},... | collective-permute-start | bytes 196616 | tf_op jit(solution)/shard_map/ppermute | solution.py:338
  46.2 8.8 %collective-permute-start.4 = (bf16[8,8,2048]{2,1,0:T(8,128)(2,1)S(1)}, bf16[8,8,2048]{2,1,0:T(8,128)(2,1)S(1)}, u32[]{:S(2)}, u32[]{:S(2)}) collective-permute-start(bf16[8,8,2048]{2,1,0:T(8,128)(2,1)S(1)} %pad_maximum_fusion.mine), channel_id=1, source_target_pairs={{16,0},{0,16},{48,32},{32,48},{80,64},{64,80},{112,96},{96,112},{1... | collective-permute-start | bytes 786440 | tf_op jit(solution)/shard_map/ppermute | solution.py:338

commit v2 on v1

--- a/solution.py
+++ b/solution.py
@@ -97,12 +97,9 @@
 
 
 def smoother():
-    band, extra = band_bins()
-    source = np.concatenate([band, extra])[:, None]
-    target = band[None, :]
-    inside = (np.abs(source - target) <= HALF) & (source >= 0)
+    band, _ = band_bins()
     counted = np.minimum(band + HALF, F - 1) - np.maximum(band - HALF, 0) + 1
-    return inside.astype(np.float32), (1.0 / counted).astype(np.float32)[None, :]
+    return np.stack([band.astype(np.float32), (1.0 / counted).astype(np.float32)])
 
 
 def phases(lags, scale):
@@ -144,7 +141,33 @@
     return low + high
 
 
-def whiten_kernel(starts, records, decimate, fourier, smooth, inverse_count, out, raw):
+def source_bins():
+    row = lax.broadcasted_iota(jnp.int32, (5 * LANES, LANES), 0)
+    within = row % LANES
+    is_band = row < FB
+    side = jnp.where(is_band, within // 64, 1 - within // 64)
+    pair = jnp.where(is_band, row // LANES, within % 64 // 8)
+    half = jnp.where(is_band, within % 64 // 32, within % 8 // 4)
+    high = jnp.where(is_band, within % 32, FB // GROUP + within % 4)
+    tile = 2 * pair + side
+    low = jnp.where(half == 0, tile, jnp.where(tile == 0, GROUP // 2, GROUP - tile))
+    used = is_band | (within % 64 < 32)
+    return jnp.where(used, GROUP * high + low, -1000).astype(jnp.float32)
+
+
+def whiten_kernel(
+    starts_hbm, records_hbm, decimate_hbm, fourier_hbm, smooth_hbm, out,
+    starts, records, decimate, fourier, smooth, raw, done,
+):
+    pairs = [
+        (starts_hbm, starts), (records_hbm, records), (decimate_hbm, decimate),
+        (fourier_hbm, fourier), (smooth_hbm, smooth),
+    ]
+    copies = [pltpu.make_async_copy(a, b, done.at[n]) for n, (a, b) in enumerate(pairs)]
+    for copy in copies:
+        copy.start()
+    copies[0].wait()
+    copies[1].wait()
     lane = lax.broadcasted_iota(jnp.int32, (PIECE, LANES), 1)
     used = 5 * GROUP + 1
     last_tile = records.shape[1] // LANES - 1
@@ -169,9 +192,11 @@
                 raw[run * 16 + w * 8 : run * 16 + w * 8 + 8, part * LANES : (part + 1) * LANES] = moved
             if part == 0 and run > 0:
                 raw[(run - 1) * 16 + w * 8 : (run - 1) * 16 + w * 8 + 8, 5 * LANES :] = moved
+    copies[2].wait()
     traces = jnp.dot(raw[...], decimate[...], precision=lax.Precision.HIGHEST, preferred_element_type=jnp.float32)
     parts = small_fourier([(traces[16 * run : 16 * run + 16], None) for run in range(GROUP)])
     left = lax.broadcasted_iota(jnp.int32, (16, LANES), 1) < 64
+    copies[3].wait()
     real_tiles, imag_tiles = [], []
     for tile in range(8):
         if tile == 0:
@@ -199,32 +224,50 @@
     rest = power - first.astype(jnp.float32)
     second = rest.astype(jnp.bfloat16)
     third = (rest - second.astype(jnp.float32)).astype(jnp.bfloat16)
+    copies[4].wait()
+    bins = source_bins()
+    window = jnp.concatenate(
+        [
+            jnp.where(jnp.abs(bins - smooth[0:1, q * LANES : (q + 1) * LANES]) <= HALF, 1.0, 0.0).astype(jnp.bfloat16)
+            for q in range(4)
+        ],
+        axis=1,
+    )
     sums = jnp.dot(
-        jnp.concatenate([first, second, third], axis=0), smooth[...], preferred_element_type=jnp.float32
+        jnp.concatenate([first, second, third], axis=0), window, preferred_element_type=jnp.float32
     )
-    smoothed = (sums[:16] + sums[16:32] + sums[32:]) * inverse_count[...]
+    smoothed = (sums[:16] + sums[16:32] + sums[32:]) * smooth[1:2, :]
     gain = lax.rsqrt(smoothed + EPS)
     for q, values in enumerate((reals, imags)):
         white = (jnp.concatenate(values, axis=1) * gain).astype(jnp.bfloat16)
         for w in range(WINDOWS):
-            out[:, (2 * w + q) * FB : (2 * w + q + 1) * FB] = white[8 * w : 8 * w + 8]
+            for copy in range(8):
+                out[copy, :, (2 * w + q) * FB : (2 * w + q + 1) * FB] = white[8 * w : 8 * w + 8]
 
 
 def whiten(records, starts):
     decimate = decimation_matrix()
     fourier = fourier_tiles()
-    smooth, inverse_count = smoother()
+    smooth = smoother()
     vmem = pl.BlockSpec(memory_space=pltpu.VMEM)
+    hbm = pl.BlockSpec(memory_space=pltpu.HBM)
     return pl.pallas_call(
         whiten_kernel,
-        out_shape=jax.ShapeDtypeStruct((PIECE, SPEC), jnp.bfloat16),
-        in_specs=[pl.BlockSpec(memory_space=pltpu.SMEM)] + [vmem] * 5,
+        out_shape=jax.ShapeDtypeStruct((8, PIECE, SPEC), jnp.bfloat16),
+        in_specs=[hbm] * 5,
         out_specs=vmem,
-        scratch_shapes=[pltpu.VMEM((16 * GROUP, 6 * LANES), jnp.float32)],
-        compiler_params=pltpu.CompilerParams(vmem_limit_bytes=32 * 1024 * 1024),
+        scratch_shapes=[
+            pltpu.SMEM((WINDOWS,), jnp.int32),
+            pltpu.VMEM(records.shape, jnp.float32),
+            pltpu.VMEM(decimate.shape, jnp.float32),
+            pltpu.VMEM(fourier.shape, jnp.float32),
+            pltpu.VMEM(smooth.shape, jnp.float32),
+            pltpu.VMEM((16 * GROUP, 6 * LANES), jnp.float32),
+            pltpu.SemaphoreType.DMA((5,)),
+        ],
+        compiler_params=pltpu.CompilerParams(vmem_limit_bytes=64 * 1024 * 1024 - 512 * 1024),
     )(
-        starts, records, jnp.asarray(decimate), jnp.asarray(fourier),
-        jnp.asarray(smooth).astype(jnp.bfloat16), jnp.asarray(inverse_count),
+        starts, records, jnp.asarray(decimate), jnp.asarray(fourier), jnp.asarray(smooth),
     )
 
 
@@ -244,35 +287,54 @@
     return values
 
 
-def correlate_kernel(places, limits, order, mine, other, receivers, fine, coarse, out, turned, spread, sources):
+def turn_kernel(own, other, fine, turned, sources):
+    core = lax.axis_index("src") % 2
+    for side, rows in enumerate((own, other)):
+
+        @pl.loop(0, 8)
+        def _(piece):
+            place = 2 * piece + (core if side == 0 else 1 - core)
+            sources[...] = rows[piece].astype(jnp.float32)
+            for pair in range(PIECE // 2):
+                for w in range(WINDOWS):
+                    at_w = 2 * w * FB
+                    reals, imags = [], []
+                    for k in range(2):
+                        ch = 2 * pair + k
+                        real = jnp.broadcast_to(sources[ch : ch + 1, at_w : at_w + FB], (FINE, FB))
+                        imag = jnp.broadcast_to(sources[ch : ch + 1, at_w + FB : at_w + 2 * FB], (FINE, FB))
+                        c, s = fine[0], fine[1]
+                        reals.append(real * c - imag * s)
+                        imags.append(real * s + imag * c)
+                    target = pl.ds(pl.multiple_of(place * PIECE * FINE + pair * 16, 16), 16)
+                    turned[target, at_w : at_w + FB] = jnp.concatenate(reals, 0).astype(jnp.bfloat16)
+                    turned[target, at_w + FB : at_w + 2 * FB] = jnp.concatenate(imags, 0).astype(jnp.bfloat16)
+
+
+def turn(own, other):
+    fine = phases(np.arange(FINE), 1.0)
+    vmem = pl.BlockSpec(memory_space=pltpu.VMEM)
+    return pl.pallas_call(
+        turn_kernel,
+        out_shape=jax.ShapeDtypeStruct((128 * FINE, SPEC), jnp.bfloat16),
+        in_specs=[vmem] * 3,
+        out_specs=vmem,
+        scratch_shapes=[pltpu.VMEM((PIECE, SPEC), jnp.float32)],
+        cost_estimate=pl.CostEstimate(flops=6 * 128 * FINE * SPEC, bytes_accessed=5 << 20, transcendentals=0),
+        compiler_params=pltpu.CompilerParams(vmem_limit_bytes=16 * 1024 * 1024),
+    )(own, other, jnp.asarray(fine))
+
+
+PER = 4
+
+
+def correlate_kernel(flip, mask, receivers, turned, coarse, *rest):
+    out, spread = rest[-2:]
     step = pl.program_id(0)
-
-    @pl.when(step == 0)
-    def _():
-        for side, rows in enumerate((mine, other)):
-
-            @pl.loop(0, 8)
-            def _(piece):
-                at = pl.multiple_of(places[side * 8 + piece] * PIECE, PIECE)
-                values = rows[piece].astype(jnp.float32)
-                sources[...] = values
-                for pair in range(PIECE // 2):
-                    for w in range(WINDOWS):
-                        at_w = 2 * w * FB
-                        reals, imags = [], []
-                        for k in range(2):
-                            ch = 2 * pair + k
-                            real = jnp.broadcast_to(sources[ch : ch + 1, at_w : at_w + FB], (FINE, FB))
-                            imag = jnp.broadcast_to(sources[ch : ch + 1, at_w + FB : at_w + 2 * FB], (FINE, FB))
-                            c, s = fine[0], fine[1]
-                            reals.append(real * c - imag * s)
-                            imags.append(real * s + imag * c)
-                        target = pl.ds(pl.multiple_of(at * FINE + pair * 16, 16), 16)
-                        turned[target, at_w : at_w + FB] = jnp.concatenate(reals, 0).astype(jnp.bfloat16)
-                        turned[target, at_w + FB : at_w + 2 * FB] = jnp.concatenate(imags, 0).astype(jnp.bfloat16)
-
-    for piece in range(2):
-        held = receivers[0, piece].astype(jnp.float32)
+    src, rcv = lax.axis_index("src"), lax.axis_index("rcv")
+    y_hi = (rcv + flip) % 2
+    for piece in range(PER):
+        held = receivers[piece].astype(jnp.float32)
         for w in range(WINDOWS):
             at_w = 2 * w * FB
             real, imag = held[:, at_w : at_w + FB], held[:, at_w + FB : at_w + 2 * FB]
@@ -289,13 +351,17 @@
                 spread[row : row + 16, at_w + FB : at_w + 2 * FB] = jnp.concatenate(imags, 0).astype(jnp.bfloat16)
 
     sublane = lax.broadcasted_iota(jnp.int32, (PIECE, LANES), 0)
+    limits = []
+    for piece in range(PER):
+        block = 2 * (PER * step + piece) + y_hi
+        limit = jnp.where(block == rcv, src * PIECE, 4096)
+        limits.append(sublane + jnp.where((block >= rcv) & (mask[block] > 0), limit, -4096))
     for chunk in range(4):
         lagged = lax.dot_general(
             spread[...], turned[chunk * 256 : (chunk + 1) * 256, :], (((1,), (1,)), ((), ())),
             preferred_element_type=jnp.float32,
         )
-        for piece in range(2):
-            limit = sublane + limits[2 * order[step] + piece]
+        for piece in range(PER):
             for half in range(2):
                 rows = piece * COARSE * PIECE
                 values = [
@@ -304,34 +370,40 @@
                 ]
                 for k, value in enumerate(swap_groups(values)):
                     source = chunk * 32 + half * 16 + k
-                    out[source, piece] = jnp.where(limit > source, value, 0.0).astype(jnp.bfloat16)
-
-
-def correlate(places, limits, order, mine, other, receivers):
-    fine = phases(np.arange(FINE), 1.0)
+                    out[source, piece, 0] = jnp.where(limits[piece] > source, value, 0.0).astype(jnp.bfloat16)
+
+
+def correlate(mask, receivers, turned, flip, result=None):
     coarse = phases(-(FINE * np.arange(COARSE) - LAGS // 2), 1.0 / math.sqrt(WINDOWS * FB))
-    whole = lambda *shape: pl.BlockSpec(shape, lambda i, *_: (0,) * len(shape))
-    grid_spec = pltpu.PrefetchScalarGridSpec(
-        num_scalar_prefetch=3,
-        grid=(8,),
-        in_specs=[
-            whole(8, PIECE, SPEC), whole(8, PIECE, SPEC),
-            pl.BlockSpec((1, 2, PIECE, SPEC), lambda i, *_: (i, 0, 0, 0)),
-            whole(2, FINE, FB), whole(2, COARSE, FB),
-        ],
-        out_specs=pl.BlockSpec((128, 2, PIECE, LAGS), lambda i, places, limits, order: (0, order[i], 0, 0)),
-        scratch_shapes=[
-            pltpu.VMEM((128 * FINE, SPEC), jnp.bfloat16),
-            pltpu.VMEM((2 * COARSE * PIECE, SPEC), jnp.bfloat16),
-            pltpu.VMEM((PIECE, SPEC), jnp.float32),
-        ],
-    )
+    vmem = pl.BlockSpec(memory_space=pltpu.VMEM)
+    operands = [mask, receivers, turned, jnp.asarray(coarse)]
+    in_specs = [
+        pl.BlockSpec(memory_space=pltpu.SMEM),
+        pl.BlockSpec((PER, PIECE, SPEC), lambda i: (i, 0, 0)),
+        vmem, vmem,
+    ]
+    aliases = {}
+    if result is not None:
+        operands.append(result)
+        in_specs.append(pl.BlockSpec(memory_space=pltpu.HBM))
+        aliases = {4: 0}
+
+    def place(i):
+        return 0, i, (lax.axis_index("rcv") + flip) % 2, 0, 0
+
     return pl.pallas_call(
-        correlate_kernel,
-        grid_spec=grid_spec,
-        out_shape=jax.ShapeDtypeStruct((128, BLOCKS, PIECE, LAGS), jnp.bfloat16),
-        compiler_params=pltpu.CompilerParams(vmem_limit_bytes=40 * 1024 * 1024),
-    )(places, limits, order, mine, other, receivers, jnp.asarray(fine), jnp.asarray(coarse))
+        functools.partial(correlate_kernel, flip),
+        grid=(8 // PER,),
+        in_specs=in_specs,
+        out_specs=pl.BlockSpec((128, PER, 1, PIECE, LAGS), place),
+        out_shape=jax.ShapeDtypeStruct((128, 8, 2, PIECE, LAGS), jnp.bfloat16),
+        scratch_shapes=[pltpu.VMEM((PER * COARSE * PIECE, SPEC), jnp.bfloat16)],
+        input_output_aliases=aliases,
+        cost_estimate=pl.CostEstimate(
+            flops=2 * 1024 * 1024 * SPEC, bytes_accessed=6 << 20, transcendentals=0
+        ),
+        compiler_params=pltpu.CompilerParams(vmem_limit_bytes=24 * 1024 * 1024),
+    )(*operands)
 
 
 def move(block, axis, source_of):
@@ -340,36 +412,15 @@
 
 def on_device(records, starts, block_mask):
     own = whiten(records, starts)
-    src = lax.axis_index("src")
-    rcv = lax.axis_index("rcv")
-    x, y_lo, core = src // 4, (src // 2) % 2, src % 2
-    z, y_hi = rcv // 2, rcv % 2
-
-    near = move(own, "src", lambda i: i ^ 2)
-    two = jnp.where(y_lo == 0, jnp.stack([own, near]), jnp.stack([near, own]))
-    mine = [two] + [
-        move(two, "src", lambda i, k=k: ((i // 4 + k) % 4) * 4 + i % 4) for k in (1, 2, 3)
-    ]
-    mine = jnp.concatenate(mine, axis=0)
+    chips = [[core + 2 * k for k in range(8)] for core in range(2)]
+    receivers = lax.all_to_all(own, "rcv", 0, 0, axis_index_groups=chips)
+    mine = lax.all_to_all(own, "src", 0, 0, axis_index_groups=chips)
     other = move(mine, "src", lambda i: i ^ 1)
-
-    far = move(own, "rcv", lambda i: i ^ 1)
-    pair = jnp.where(y_hi == 0, jnp.stack([own, far]), jnp.stack([far, own]))
-    pairs = [pair] + [
-        move(pair, "rcv", lambda i, k=k: ((i // 2 + k) % 8) * 2 + i % 2) for k in range(1, 8)
-    ]
-    receivers = jnp.stack(pairs)
-
-    k = jnp.arange(8, dtype=jnp.int32)
-    chip = ((x + k // 2) % 4) * 4 + (k % 2) * 2
-    places = jnp.concatenate([chip + core, chip + 1 - core])
-    order = (z + k) % 8
-    pieces = jnp.arange(BLOCKS, dtype=jnp.int32)
-    wanted = block_mask.reshape(-1) > 0
-    limits = jnp.where(
-        wanted & (pieces >= rcv), jnp.where(pieces == rcv, src * PIECE, 4096), -4096
-    ).astype(jnp.int32)
-    result = correlate(places, limits, order, mine, other, receivers)
+    turned = turn(mine, other)
+    far = move(receivers, "rcv", lambda i: i ^ 1)
+    mask = block_mask.reshape(-1)
+    result = correlate(mask, receivers, turned, 0)
+    result = correlate(mask, far, turned, 1, result)
     return result.reshape(128, BLOCKS, 1, PIECE, LAGS)
 
 

time: 71.5 us -> 56 us (0.78)
  the two profiles are of different devices: /device:TPU:1 before, /device:TPU:8 now
where the time goes in v2:
time: 56 us; the launch traced here: 55.7 us
  Pallas kernels  22.3 us (40%)
  blocking collectives  11.9 us (21%)
  starting transfers between devices  10.8 us (19%)
  waiting for transfers between devices  10.7 us (19%)
    pallas_call x2, Pallas kernels, correlate(): pl.pallas_call(functools.partial(correlate_kernel, flip), grid=(8 // PER,...  15.4 us
    all_to_all x1, blocking collectives, on_device(): mine = lax.all_to_all(own, 'src', 0, 0, axis_index_groups=chips)  11.9 us
    all_to_all x1, waiting for transfers between devices, on_device(): receivers = lax.all_to_all(own, 'rcv', 0, 0, axis_index_groups=chips)  10.7 us
    all_to_all x1, starting transfers between devices, on_device(): receivers = lax.all_to_all(own, 'rcv', 0, 0, axis_index_groups=chips)  8.46 us
    pallas_call x1, Pallas kernels, whiten(): pl.pallas_call(whiten_kernel, out_shape=jax.ShapeDtypeStruct((8, PIECE, S...  5.69 us
    ppermute x2, starting transfers between devices, move(): lax.ppermute(block, axis, [(source_of(i), i) for i in range(lax.axis_size...  2.3 us
    pallas_call x1, Pallas kernels, turn(): pl.pallas_call(turn_kernel, out_shape=jax.ShapeDtypeStruct((128 * FINE, S...  1.18 us
  transfers between devices with their start and end apart: 3, of which 1 were waited for; matrix products, arithmetic and copies ran while one was open for 0% of the time, Pallas kernels for 16%

profile of v2, /device:TPU:8, one launch (start us, length us, event | category | flops | bytes accessed | tf_op | source)
XLA Modules:
  0.0 55.7 jit_solution(14996646107286319009)
XLA Ops:
  0.0 0.0 copy-start
  0.0 0.0 copy-start.2
  0.0 0.0 copy-start.1
  0.0 5.7 %shard_map.91 = bf16[8,8,2048]{2,1,0:T(8,128)(2,1)} custom-call(s32[2]{0:T(128)} %starts_hbm.1, f32[8,20480]{1,0:T(8,128)} %records_hbm.1, f32[768,128]{1,0:T(8,128)} %constant.10.clone.decimate_hbm, f32[8,256,256]{2,1,0:T(8,128)} %constant.11.clone.fourier_hbm, f32[2,512]{1,0:T(2,128)} %constant.12.clone.smooth_hbm), custom_call_target="tpu_custom_call" | custom-call | tf_op jit(solution)/shard_map/pallas_call | solution.py:254
  5.7 11.9 %all_to_all.10.own = bf16[8,8,2048]{2,1,0:T(8,128)(2,1)S(1)} all-to-all(bf16[8,8,2048]{2,1,0:T(8,128)(2,1)} %shard_map.91), channel_id=1, replica_groups={{0,32,64,96,128,160,192,224},{16,48,80,112,144,176,208,240},{1,33,65,97..., dimensions={0} | all-to-all | bytes 524288 | tf_op jit(solution)/shard_map/all_to_all | solution.py:417
  17.6 8.5 %all-to-all-start = ((bf16[8,8,2048]{2,1,0:T(8,128)(2,1)}), bf16[8,8,2048]{2,1,0:T(8,128)(2,1)S(1)}, u32[]{:S(2)}, u32[]{:S(2)}) async-start(bf16[8,8,2048]{2,1,0:T(8,128)(2,1)} %shard_map.91), calls=%async_computation | async-start | bytes 524288 | tf_op jit(solution)/shard_map/all_to_all | solution.py:416
  26.1 0.0 collective-permute-start.1
  26.1 10.7 %all-to-all-done.receivers = bf16[8,8,2048]{2,1,0:T(8,128)(2,1)S(1)} async-done(((bf16[8,8,2048]{2,1,0:T(8,128)(2,1)}), bf16[8,8,2048]{2,1,0:T(8,128)(2,1)S(1)}, u32[]{:S(2)}, u32[]{:S(2)}) %all-to-all-start) | async-done | bytes 262176 | tf_op jit(solution)/shard_map/all_to_all | solution.py:416
  36.8 2.3 %collective-permute-start = (bf16[8,8,2048]{2,1,0:T(8,128)(2,1)S(1)}, bf16[8,8,2048]{2,1,0:T(8,128)(2,1)S(1)}, u32[]{:S(2)}, u32[]{:S(2)}) collective-permute-start(bf16[8,8,2048]{2,1,0:T(8,128)(2,1)S(1)} %all-to-all-done.receivers), channel_id=1, source_target_pairs={{1,0},{0,1},{3,2},{2,3},{5,4},{4,5},{7,6},{6,7},{9,8},{8,9},{11,10... | collective-permute-start | bytes 786440 | tf_op jit(solution)/shard_map/ppermute | solution.py:410
  39.1 0.0 collective-permute-done.1.other
  39.1 0.0 copy-done
  39.1 1.2 %shard_map.92.turned = bf16[1024,2048]{1,0:T(8,128)(2,1)S(1)} custom-call(bf16[8,8,2048]{2,1,0:T(8,128)(2,1)S(1)} %all_to_all.10.own, bf16[8,8,2048]{2,1,0:T(8,128)(2,1)S(1)} %collective-permute-done.1.other, f32[2,8,512]{2,1,0:T(8,128)S(1)} %copy-done), custom_call_target="tpu_custom_call" | custom-call | flops 12582912 | bytes 5242880 | tf_op jit(solution)/shard_map/pallas_call | solution.py:317
  40.3 0.0 copy-done.2
  40.3 0.0 copy-done.1
  40.3 7.7 %shard_map.93.rest_0_ = bf16[128,8,2,8,128]{4,3,2,1,0:T(8,128)(2,1)} custom-call(s32[16]{0:T(128)S(1)} %bitcast.4, bf16[8,8,2048]{2,1,0:T(8,128)(2,1)S(1)} %all-to-all-done.receivers, bf16[1024,2048]{1,0:T(8,128)(2,1)S(1)} %shard_map.92.turned, f32[2,16,512]{2,1,0:T(8,128)S(1)} %copy-done.2), custom_call_target="tpu_custom_call" | custom-call | flops 4294967296 | bytes 6291456 | tf_op jit(solution)/shard_map/pallas_call | solution.py:394
  48.0 0.0 collective-permute-done.receivers
  48.0 7.7 %shard_map.94 = bf16[128,8,2,8,128]{4,3,2,1,0:T(8,128)(2,1)} custom-call(s32[16]{0:T(128)S(1)} %bitcast.5, bf16[8,8,2048]{2,1,0:T(8,128)(2,1)S(1)} %collective-permute-done.receivers, bf16[1024,2048]{1,0:T(8,128)(2,1)S(1)} %shard_map.92.turned, f32[2,16,512]{2,1,0:T(8,128)S(1)} %copy-done.2, ...), custom_call_target="tpu_custom_call", output_to_operand_aliasing={{}: (4, {})} | custom-call | flops 4294967296 | bytes 6291456 | tf_op jit(solution)/shard_map/pallas_call | solution.py:394
Async XLA Ops:
  0.0 39.1 %copy-start = (f32[2,8,512]{2,1,0:T(8,128)S(1)}, f32[2,8,512]{2,1,0:T(8,128)}, u32[]{:S(2)}) copy-start(f32[2,8,512]{2,1,0:T(8,128)} %constant.13.clone.fine) | copy-start | bytes 98308
  0.0 40.3 %copy-start.2 = (f32[2,16,512]{2,1,0:T(8,128)S(1)}, f32[2,16,512]{2,1,0:T(8,128)}, u32[]{:S(2)}) copy-start(f32[2,16,512]{2,1,0:T(8,128)} %constant.14.clone.coarse) | copy-start | bytes 196612
  0.0 40.3 %copy-start.1 = (s32[1,16,1]{1,2,0:T(1,128)S(1)}, s32[1,16,1]{1,2,0:T(1,128)}, u32[]{:S(2)}) copy-start(s32[1,16,1]{1,2,0:T(1,128)} %param.11) | copy-start | bytes 196
  17.6 19.2 %all-to-all-start = ((bf16[8,8,2048]{2,1,0:T(8,128)(2,1)}), bf16[8,8,2048]{2,1,0:T(8,128)(2,1)S(1)}, u32[]{:S(2)}, u32[]{:S(2)}) async-start(bf16[8,8,2048]{2,1,0:T(8,128)(2,1)} %shard_map.91), calls=%async_computation | async-start | bytes 524288 | tf_op jit(solution)/shard_map/all_to_all | solution.py:416
  26.1 13.0 %collective-permute-start.1 = (bf16[8,8,2048]{2,1,0:T(8,128)(2,1)S(1)}, bf16[8,8,2048]{2,1,0:T(8,128)(2,1)S(1)}, u32[]{:S(2)}, u32[]{:S(2)}) collective-permute-start(bf16[8,8,2048]{2,1,0:T(8,128)(2,1)S(1)} %all_to_all.10.own), channel_id=1, source_target_pairs={{16,0},{0,16},{48,32},{32,48},{80,64},{64,80},{112,96},{96,112},{1... | collective-permute-start | bytes 786440 | tf_op jit(solution)/shard_map/ppermute | solution.py:410
  36.8 11.2 %collective-permute-start = (bf16[8,8,2048]{2,1,0:T(8,128)(2,1)S(1)}, bf16[8,8,2048]{2,1,0:T(8,128)(2,1)S(1)}, u32[]{:S(2)}, u32[]{:S(2)}) collective-permute-start(bf16[8,8,2048]{2,1,0:T(8,128)(2,1)S(1)} %all-to-all-done.receivers), channel_id=1, source_target_pairs={{1,0},{0,1},{3,2},{2,3},{5,4},{4,5},{7,6},{6,7},{9,8},{8,9},{11,10... | collective-permute-start | bytes 786440 | tf_op jit(solution)/shard_map/ppermute | solution.py:410

commit v3 on v2

--- a/solution.py
+++ b/solution.py
@@ -156,7 +156,7 @@
 
 
 def whiten_kernel(
-    starts_hbm, records_hbm, decimate_hbm, fourier_hbm, smooth_hbm, out,
+    starts_hbm, records_hbm, decimate_hbm, fourier_hbm, smooth_hbm, out, out_one,
     starts, records, decimate, fourier, smooth, raw, done,
 ):
     pairs = [
@@ -241,6 +241,7 @@
     for q, values in enumerate((reals, imags)):
         white = (jnp.concatenate(values, axis=1) * gain).astype(jnp.bfloat16)
         for w in range(WINDOWS):
+            out_one[:, (2 * w + q) * FB : (2 * w + q + 1) * FB] = white[8 * w : 8 * w + 8]
             for copy in range(8):
                 out[copy, :, (2 * w + q) * FB : (2 * w + q + 1) * FB] = white[8 * w : 8 * w + 8]
 
@@ -253,9 +254,12 @@
     hbm = pl.BlockSpec(memory_space=pltpu.HBM)
     return pl.pallas_call(
         whiten_kernel,
-        out_shape=jax.ShapeDtypeStruct((8, PIECE, SPEC), jnp.bfloat16),
+        out_shape=(
+            jax.ShapeDtypeStruct((8, PIECE, SPEC), jnp.bfloat16),
+            jax.ShapeDtypeStruct((PIECE, SPEC), jnp.bfloat16),
+        ),
         in_specs=[hbm] * 5,
-        out_specs=vmem,
+        out_specs=(vmem, vmem),
         scratch_shapes=[
             pltpu.SMEM((WINDOWS,), jnp.int32),
             pltpu.VMEM(records.shape, jnp.float32),
@@ -287,13 +291,14 @@
     return values
 
 
-def turn_kernel(own, other, fine, turned, sources):
-    core = lax.axis_index("src") % 2
+def turn_sources(own, other, fine, turned, sources):
+    src = lax.axis_index("src")
+    x, core = src // 4, src % 2
     for side, rows in enumerate((own, other)):
 
         @pl.loop(0, 8)
         def _(piece):
-            place = 2 * piece + (core if side == 0 else 1 - core)
+            place = (x + piece // 2) % 4 * 4 + piece % 2 * 2 + (core if side == 0 else 1 - core)
             sources[...] = rows[piece].astype(jnp.float32)
             for pair in range(PIECE // 2):
                 for w in range(WINDOWS):
@@ -311,26 +316,20 @@
                     turned[target, at_w + FB : at_w + 2 * FB] = jnp.concatenate(imags, 0).astype(jnp.bfloat16)
 
 
-def turn(own, other):
-    fine = phases(np.arange(FINE), 1.0)
-    vmem = pl.BlockSpec(memory_space=pltpu.VMEM)
-    return pl.pallas_call(
-        turn_kernel,
-        out_shape=jax.ShapeDtypeStruct((128 * FINE, SPEC), jnp.bfloat16),
-        in_specs=[vmem] * 3,
-        out_specs=vmem,
-        scratch_shapes=[pltpu.VMEM((PIECE, SPEC), jnp.float32)],
-        cost_estimate=pl.CostEstimate(flops=6 * 128 * FINE * SPEC, bytes_accessed=5 << 20, transcendentals=0),
-        compiler_params=pltpu.CompilerParams(vmem_limit_bytes=16 * 1024 * 1024),
-    )(own, other, jnp.asarray(fine))
-
-
 PER = 4
 
 
-def correlate_kernel(flip, mask, receivers, turned, coarse, *rest):
-    out, spread = rest[-2:]
+def correlate_kernel(flip, mask, receivers, coarse, *rest):
     step = pl.program_id(0)
+    if flip:
+        turned, _, out, spread = rest
+    else:
+        own, other, fine, out, turned, spread, sources = rest
+
+        @pl.when(step == 0)
+        def _():
+            turn_sources(own, other, fine, turned, sources)
+
     src, rcv = lax.axis_index("src"), lax.axis_index("rcv")
     y_hi = (rcv + flip) % 2
     for piece in range(PER):
@@ -373,54 +372,75 @@
                     out[source, piece, 0] = jnp.where(limits[piece] > source, value, 0.0).astype(jnp.bfloat16)
 
 
-def correlate(mask, receivers, turned, flip, result=None):
+def correlate(mask, receivers, flip, *rest):
+    fine = phases(np.arange(FINE), 1.0)
     coarse = phases(-(FINE * np.arange(COARSE) - LAGS // 2), 1.0 / math.sqrt(WINDOWS * FB))
     vmem = pl.BlockSpec(memory_space=pltpu.VMEM)
-    operands = [mask, receivers, turned, jnp.asarray(coarse)]
+
+    def place(i):
+        return 0, i, (lax.axis_index("rcv") + flip) % 2, 0, 0
+
     in_specs = [
         pl.BlockSpec(memory_space=pltpu.SMEM),
         pl.BlockSpec((PER, PIECE, SPEC), lambda i: (i, 0, 0)),
-        vmem, vmem,
+        vmem,
     ]
-    aliases = {}
-    if result is not None:
-        operands.append(result)
-        in_specs.append(pl.BlockSpec(memory_space=pltpu.HBM))
-        aliases = {4: 0}
-
-    def place(i):
-        return 0, i, (lax.axis_index("rcv") + flip) % 2, 0, 0
-
-    return pl.pallas_call(
-        functools.partial(correlate_kernel, flip),
+    result = jax.ShapeDtypeStruct((128, 8, 2, PIECE, LAGS), jnp.bfloat16)
+    turned = jax.ShapeDtypeStruct((128 * FINE, SPEC), jnp.bfloat16)
+    block = pl.BlockSpec((128, PER, 1, PIECE, LAGS), place)
+    spread = pltpu.VMEM((PER * COARSE * PIECE, SPEC), jnp.bfloat16)
+    common = dict(
         grid=(8 // PER,),
-        in_specs=in_specs,
-        out_specs=pl.BlockSpec((128, PER, 1, PIECE, LAGS), place),
-        out_shape=jax.ShapeDtypeStruct((128, 8, 2, PIECE, LAGS), jnp.bfloat16),
-        scratch_shapes=[pltpu.VMEM((PER * COARSE * PIECE, SPEC), jnp.bfloat16)],
-        input_output_aliases=aliases,
         cost_estimate=pl.CostEstimate(
             flops=2 * 1024 * 1024 * SPEC, bytes_accessed=6 << 20, transcendentals=0
         ),
         compiler_params=pltpu.CompilerParams(vmem_limit_bytes=24 * 1024 * 1024),
-    )(*operands)
+    )
+    operands = (mask, receivers, jnp.asarray(coarse)) + rest
+    if flip:
+        return pl.pallas_call(
+            functools.partial(correlate_kernel, flip),
+            in_specs=in_specs + [vmem, pl.BlockSpec(memory_space=pltpu.HBM)],
+            out_specs=block, out_shape=result, scratch_shapes=[spread],
+            input_output_aliases={4: 0}, **common,
+        )(*operands)
+    return pl.pallas_call(
+        functools.partial(correlate_kernel, flip),
+        in_specs=in_specs + [vmem] * 3,
+        out_specs=(block, vmem), out_shape=(result, turned),
+        scratch_shapes=[spread, pltpu.VMEM((PIECE, SPEC), jnp.float32)], **common,
+    )(*operands, jnp.asarray(fine))
 
 
 def move(block, axis, source_of):
     return lax.ppermute(block, axis, [(source_of(i), i) for i in range(lax.axis_size(axis))])
 
 
+CHIPS = [[core + 2 * k for k in range(8)] for core in range(2)]
+
+
+def gather_sources(own, near):
+    y_lo = lax.axis_index("src") // 2 % 2
+    two = jnp.where(y_lo == 0, jnp.stack([own, near]), jnp.stack([near, own]))
+    mine = jnp.concatenate([two] + [
+        move(two, "src", lambda i, k=k: ((i // 4 + k) % 4) * 4 + i % 4) for k in (1, 2, 3)
+    ])
+    return mine, move(mine, "src", lambda i: i ^ 1)
+
+
+def no_sources(own, near):
+    return (jnp.zeros((8, PIECE, SPEC), own.dtype),) * 2
+
+
 def on_device(records, starts, block_mask):
-    own = whiten(records, starts)
-    chips = [[core + 2 * k for k in range(8)] for core in range(2)]
-    receivers = lax.all_to_all(own, "rcv", 0, 0, axis_index_groups=chips)
-    mine = lax.all_to_all(own, "src", 0, 0, axis_index_groups=chips)
-    other = move(mine, "src", lambda i: i ^ 1)
-    turned = turn(mine, other)
+    copies, own = whiten(records, starts)
+    near = move(own, "src", lambda i: i ^ 2)
+    receivers = lax.all_to_all(copies, "rcv", 0, 0, axis_index_groups=CHIPS)
+    mine, other = lax.cond(starts[0] >= 0, gather_sources, no_sources, own, near)
     far = move(receivers, "rcv", lambda i: i ^ 1)
     mask = block_mask.reshape(-1)
-    result = correlate(mask, receivers, turned, 0)
-    result = correlate(mask, far, turned, 1, result)
+    result, turned = correlate(mask, receivers, 0, mine, other)
+    result = correlate(mask, far, 1, turned, result)
     return result.reshape(128, BLOCKS, 1, PIECE, LAGS)
 
 

time: 56 us -> 50.8 us (0.907)
  the two profiles are of different devices: /device:TPU:8 before, /device:TPU:1 now
where the time goes in v3:
time: 50.8 us; the launch traced here: 50.5 us
  Pallas kernels  22.9 us (45%)
  starting transfers between devices  21.6 us (43%)
  waiting for transfers between devices  4.58 us (9%)
  other arithmetic  0.75 us (1%)
  between operations  0.67 us (1%)
    pallas_call x2, Pallas kernels, correlate(): pl.pallas_call(functools.partial(correlate_kernel, flip), in_specs=in_spe...  17.2 us
    ppermute x6, starting transfers between devices, move(): lax.ppermute(block, axis, [(source_of(i), i) for i in range(lax.axis_size...  12.6 us
    all_to_all x1, starting transfers between devices, on_device(): receivers = lax.all_to_all(copies, 'rcv', 0, 0, axis_index_groups=CHIPS)  9.03 us
    pallas_call x1, Pallas kernels, whiten(): pl.pallas_call(whiten_kernel, out_shape=(jax.ShapeDtypeStruct((8, PIECE,...  5.69 us
    ppermute x6, waiting for transfers between devices, move(): lax.ppermute(block, axis, [(source_of(i), i) for i in range(lax.axis_size...  4.58 us
  transfers between devices with their start and end apart: 7, of which 4 were waited for; matrix products, arithmetic and copies ran while one was open for 1% of the time, Pallas kernels for 19%

profile of v3, /device:TPU:1, one launch (start us, length us, event | category | flops | bytes accessed | tf_op | source)
XLA Modules:
  0.0 50.5 jit_solution(10803276101541417173)
XLA Ops:
  0.0 0.0 copy-start.1
  0.0 0.0 copy-start.2
  0.0 0.0 copy-start
  0.0 5.7 %shard_map.91 = (bf16[8,8,2048]{2,1,0:T(8,128)(2,1)}, bf16[8,2048]{1,0:T(8,128)(2,1)S(1)}) custom-call(s32[2]{0:T(128)} %starts_hbm.1, f32[8,20480]{1,0:T(8,128)} %records_hbm.1, f32[768,128]{1,0:T(8,128)} %constant.45.clone.decimate_hbm, f32[8,256,256]{2,1,0:T(8,128)} %constant.46.clone.fourier_hbm, f32[2,512]{1,0:T(2,128)} %constant.47.clone.smooth_hbm), custom_call_target="tpu_custom_call" | custom-call | tf_op jit(solution)/shard_map/pallas_call | solution.py:255
  5.7 9.0 %all-to-all-start = ((bf16[8,8,2048]{2,1,0:T(8,128)(2,1)}), bf16[8,8,2048]{2,1,0:T(8,128)(2,1)S(1)}, u32[]{:S(2)}, u32[]{:S(2)}) async-start(bf16[8,8,2048]{2,1,0:T(8,128)(2,1)} %get-tuple-element.17), calls=%async_computation | async-start | bytes 524288 | tf_op jit(solution)/shard_map/all_to_all | solution.py:438
  14.7 1.3 %collective-permute-start.5 = (bf16[8,2048]{1,0:T(8,128)(2,1)S(1)}, bf16[8,2048]{1,0:T(8,128)(2,1)S(1)}, u32[]{:S(2)}, u32[]{:S(2)}) collective-permute-start(bf16[8,2048]{1,0:T(8,128)(2,1)S(1)} %get-tuple-element.18), channel_id=1, source_target_pairs={{32,0},{48,16},{0,32},{16,48},{96,64},{112,80},{64,96},{80,112},{1... | collective-permute-start | bytes 98312 | tf_op jit(solution)/shard_map/ppermute | solution.py:416
  16.7 0.8 %collective-permute-done.5 = bf16[8,2048]{1,0:T(8,128)(2,1)S(1)} collective-permute-done((bf16[8,2048]{1,0:T(8,128)(2,1)S(1)}, bf16[8,2048]{1,0:T(8,128)(2,1)S(1)}, u32[]{:S(2)}, u32[]{:S(2)}) %collective-permute-start.5) | collective-permute-done | bytes 32800 | tf_op jit(solution)/shard_map/ppermute | solution.py:416
  17.5 12.9 %conditional.1 = (bf16[8,8,2048]{2,1,0:T(8,128)(2,1)}, bf16[8,8,2048]{2,1,0:T(8,128)(2,1)}) conditional(s32[]{:T(128)} %bitcast.3, () %tuple.13, (bf16[8,2048]{1,0:T(8,128)(2,1)S(1)}, bf16[8,2048]{1,0:T(8,128)(2,1)S(1)}) %tuple.14), branch_computations={%region_0.0_spmd, %region_1.2_spmd} | conditional | flops 491550 | bytes 2490845 | solution.py:439
  17.5 1.3 %collective-permute-start.2 = (bf16[2,8,2048]{2,1,0:T(8,128)(2,1)S(1)}, bf16[2,8,2048]{2,1,0:T(8,128)(2,1)S(1)}, u32[]{:S(2)}, u32[]{:S(2)}) collective-permute-start(bf16[2,8,2048]{2,1,0:T(8,128)(2,1)S(1)} %maximum_select_fusion), channel_id=1, source_target_pairs={{192,0},{208,16},{224,32},{240,48},{0,64},{16,80},{32,96},{48,112}... | collective-permute-start | bytes 196616 | tf_op jit(solution)/shard_map/cond/branch_1_fun/ppermute | solution.py:416
  18.8 2.5 %collective-permute-start.1 = (bf16[2,8,2048]{2,1,0:T(8,128)(2,1)S(1)}, bf16[2,8,2048]{2,1,0:T(8,128)(2,1)S(1)}, u32[]{:S(2)}, u32[]{:S(2)}) collective-permute-start(bf16[2,8,2048]{2,1,0:T(8,128)(2,1)S(1)} %maximum_select_fusion), channel_id=1, source_target_pairs={{128,0},{144,16},{160,32},{176,48},{192,64},{208,80},{224,96},{240... | collective-permute-start | bytes 196616 | tf_op jit(solution)/shard_map/cond/branch_1_fun/ppermute | solution.py:416
  21.3 1.1 %collective-permute-start = (bf16[2,8,2048]{2,1,0:T(8,128)(2,1)S(1)}, bf16[2,8,2048]{2,1,0:T(8,128)(2,1)S(1)}, u32[]{:S(2)}, u32[]{:S(2)}) collective-permute-start(bf16[2,8,2048]{2,1,0:T(8,128)(2,1)S(1)} %maximum_select_fusion), channel_id=1, source_target_pairs={{64,0},{80,16},{96,32},{112,48},{128,64},{144,80},{160,96},{176,11... | collective-permute-start | bytes 196616 | tf_op jit(solution)/shard_map/cond/branch_1_fun/ppermute | solution.py:416
  22.4 0.0 collective-permute-done.2
  22.4 1.2 %collective-permute-done.1 = bf16[2,8,2048]{2,1,0:T(8,128)(2,1)S(1)} collective-permute-done((bf16[2,8,2048]{2,1,0:T(8,128)(2,1)S(1)}, bf16[2,8,2048]{2,1,0:T(8,128)(2,1)S(1)}, u32[]{:S(2)}, u32[]{:S(2)}) %collective-permute-start.1) | collective-permute-done | bytes 65568 | tf_op jit(solution)/shard_map/cond/branch_1_fun/ppermute | solution.py:416
  23.6 1.1 %collective-permute-done = bf16[2,8,2048]{2,1,0:T(8,128)(2,1)S(1)} collective-permute-done((bf16[2,8,2048]{2,1,0:T(8,128)(2,1)S(1)}, bf16[2,8,2048]{2,1,0:T(8,128)(2,1)S(1)}, u32[]{:S(2)}, u32[]{:S(2)}) %collective-permute-start) | collective-permute-done | bytes 65568 | tf_op jit(solution)/shard_map/cond/branch_1_fun/ppermute | solution.py:416
  24.7 0.7 %pad_maximum_fusion = bf16[8,8,2048]{2,1,0:T(8,128)(2,1)} fusion(bf16[2,8,2048]{2,1,0:T(8,128)(2,1)S(1)} %collective-permute-done.2, bf16[2,8,2048]{2,1,0:T(8,128)(2,1)S(1)} %collective-permute-done.1, bf16[2,8,2048]{2,1,0:T(8,128)(2,1)S(1)} %collective-permute-done, bf16[2,8,2048]{2,1,0:T(8,128)(2,1)S(1)} %maximum_select_fusion), kind=kLoop, calls=%fused_computation | loop fusion | flops 393216 | bytes 524288 | tf_op jit(solution)/shard_map/cond/branch_1_fun/concatenate | solution.py:425
  25.4 3.5 %collective-permute-start.3 = (bf16[8,8,2048]{2,1,0:T(8,128)(2,1)}, bf16[8,8,2048]{2,1,0:T(8,128)(2,1)}, u32[]{:S(2)}, u32[]{:S(2)}) collective-permute-start(bf16[8,8,2048]{2,1,0:T(8,128)(2,1)} %pad_maximum_fusion), channel_id=1, source_target_pairs={{16,0},{0,16},{48,32},{32,48},{80,64},{64,80},{112,96},{96,112},{1... | collective-permute-start | bytes 786440 | tf_op jit(solution)/shard_map/cond/branch_1_fun/ppermute | solution.py:416
  28.9 1.5 %collective-permute-done.3 = bf16[8,8,2048]{2,1,0:T(8,128)(2,1)} collective-permute-done((bf16[8,8,2048]{2,1,0:T(8,128)(2,1)}, bf16[8,8,2048]{2,1,0:T(8,128)(2,1)}, u32[]{:S(2)}, u32[]{:S(2)}) %collective-permute-start.3) | collective-permute-done | bytes 262176 | tf_op jit(solution)/shard_map/cond/branch_1_fun/ppermute | solution.py:416
  30.4 0.0 all-to-all-done.receivers
  30.4 2.9 %collective-permute-start.4 = (bf16[8,8,2048]{2,1,0:T(8,128)(2,1)S(1)}, bf16[8,8,2048]{2,1,0:T(8,128)(2,1)S(1)}, u32[]{:S(2)}, u32[]{:S(2)}) collective-permute-start(bf16[8,8,2048]{2,1,0:T(8,128)(2,1)S(1)} %all-to-all-done.receivers), channel_id=1, source_target_pairs={{1,0},{0,1},{3,2},{2,3},{5,4},{4,5},{7,6},{6,7},{9,8},{8,9},{11,10... | collective-permute-start | bytes 786440 | tf_op jit(solution)/shard_map/ppermute | solution.py:416
  33.4 0.0 copy-done.1
  33.4 0.0 copy-done.2
  33.4 0.0 copy-done
  33.4 9.5 %shard_map.92 = (bf16[128,8,2,8,128]{4,3,2,1,0:T(8,128)(2,1)}, bf16[1024,2048]{1,0:T(8,128)(2,1)S(1)}) custom-call(s32[16]{0:T(128)S(1)} %bitcast.8, bf16[8,8,2048]{2,1,0:T(8,128)(2,1)S(1)} %all-to-all-done.receivers, f32[2,16,512]{2,1,0:T(8,128)S(1)} %copy-done.1, bf16[8,8,2048]{2,1,0:T(8,128)(2,1)} %get-tuple-element.19.rest_0_, ...), custom_call_target="tpu_custom_call" | custom-call | flops 4294967296 | bytes 6291456 | tf_op jit(solution)/shard_map/pallas_call | solution.py:407
  42.8 0.0 collective-permute-done.4.receivers
  42.8 7.7 %shard_map.93 = bf16[128,8,2,8,128]{4,3,2,1,0:T(8,128)(2,1)} custom-call(s32[16]{0:T(128)S(1)} %bitcast.9, bf16[8,8,2048]{2,1,0:T(8,128)(2,1)S(1)} %collective-permute-done.4.receivers, f32[2,16,512]{2,1,0:T(8,128)S(1)} %copy-done.1, bf16[1024,2048]{1,0:T(8,128)(2,1)S(1)} %get-tuple-element.21.rest_0_, ...), custom_call_target="tpu_custom_call", output_to_operand_aliasing={{}: (4, {})} | custom-call | flops 4294967296 | bytes 6291456 | tf_op jit(solution)/shard_map/pallas_call | solution.py:401
  (1 shorter events, 0.0 us)
Async XLA Ops:
  0.0 33.4 %copy-start.1 = (f32[2,16,512]{2,1,0:T(8,128)S(1)}, f32[2,16,512]{2,1,0:T(8,128)}, u32[]{:S(2)}) copy-start(f32[2,16,512]{2,1,0:T(8,128)} %constant.48.clone.coarse) | copy-start | bytes 196612
  0.0 33.4 %copy-start.2 = (f32[2,8,512]{2,1,0:T(8,128)S(1)}, f32[2,8,512]{2,1,0:T(8,128)}, u32[]{:S(2)}) copy-start(f32[2,8,512]{2,1,0:T(8,128)} %constant.49.clone.rest_2_) | copy-start | bytes 98308
  0.0 33.4 %copy-start = (s32[1,16,1]{1,2,0:T(1,128)S(1)}, s32[1,16,1]{1,2,0:T(1,128)}, u32[]{:S(2)}) copy-start(s32[1,16,1]{1,2,0:T(1,128)} %param.13) | copy-start | bytes 196
  5.7 24.7 %all-to-all-start = ((bf16[8,8,2048]{2,1,0:T(8,128)(2,1)}), bf16[8,8,2048]{2,1,0:T(8,128)(2,1)S(1)}, u32[]{:S(2)}, u32[]{:S(2)}) async-start(bf16[8,8,2048]{2,1,0:T(8,128)(2,1)} %get-tuple-element.17), calls=%async_computation | async-start | bytes 524288 | tf_op jit(solution)/shard_map/all_to_all | solution.py:438
  14.7 2.8 %collective-permute-start.5 = (bf16[8,2048]{1,0:T(8,128)(2,1)S(1)}, bf16[8,2048]{1,0:T(8,128)(2,1)S(1)}, u32[]{:S(2)}, u32[]{:S(2)}) collective-permute-start(bf16[8,2048]{1,0:T(8,128)(2,1)S(1)} %get-tuple-element.18), channel_id=1, source_target_pairs={{32,0},{48,16},{0,32},{16,48},{96,64},{112,80},{64,96},{80,112},{1... | collective-permute-start | bytes 98312 | tf_op jit(solution)/shard_map/ppermute | solution.py:416
  17.5 4.9 %collective-permute-start.2 = (bf16[2,8,2048]{2,1,0:T(8,128)(2,1)S(1)}, bf16[2,8,2048]{2,1,0:T(8,128)(2,1)S(1)}, u32[]{:S(2)}, u32[]{:S(2)}) collective-permute-start(bf16[2,8,2048]{2,1,0:T(8,128)(2,1)S(1)} %maximum_select_fusion), channel_id=1, source_target_pairs={{192,0},{208,16},{224,32},{240,48},{0,64},{16,80},{32,96},{48,112}... | collective-permute-start | bytes 196616 | tf_op jit(solution)/shard_map/cond/branch_1_fun/ppermute | solution.py:416
  18.8 4.8 %collective-permute-start.1 = (bf16[2,8,2048]{2,1,0:T(8,128)(2,1)S(1)}, bf16[2,8,2048]{2,1,0:T(8,128)(2,1)S(1)}, u32[]{:S(2)}, u32[]{:S(2)}) collective-permute-start(bf16[2,8,2048]{2,1,0:T(8,128)(2,1)S(1)} %maximum_select_fusion), channel_id=1, source_target_pairs={{128,0},{144,16},{160,32},{176,48},{192,64},{208,80},{224,96},{240... | collective-permute-start | bytes 196616 | tf_op jit(solution)/shard_map/cond/branch_1_fun/ppermute | solution.py:416
  21.3 3.4 %collective-permute-start = (bf16[2,8,2048]{2,1,0:T(8,128)(2,1)S(1)}, bf16[2,8,2048]{2,1,0:T(8,128)(2,1)S(1)}, u32[]{:S(2)}, u32[]{:S(2)}) collective-permute-start(bf16[2,8,2048]{2,1,0:T(8,128)(2,1)S(1)} %maximum_select_fusion), channel_id=1, source_target_pairs={{64,0},{80,16},{96,32},{112,48},{128,64},{144,80},{160,96},{176,11... | collective-permute-start | bytes 196616 | tf_op jit(solution)/shard_map/cond/branch_1_fun/ppermute | solution.py:416
  25.4 5.0 %collective-permute-start.3 = (bf16[8,8,2048]{2,1,0:T(8,128)(2,1)}, bf16[8,8,2048]{2,1,0:T(8,128)(2,1)}, u32[]{:S(2)}, u32[]{:S(2)}) collective-permute-start(bf16[8,8,2048]{2,1,0:T(8,128)(2,1)} %pad_maximum_fusion), channel_id=1, source_target_pairs={{16,0},{0,16},{48,32},{32,48},{80,64},{64,80},{112,96},{96,112},{1... | collective-permute-start | bytes 786440 | tf_op jit(solution)/shard_map/cond/branch_1_fun/ppermute | solution.py:416
  30.4 12.4 %collective-permute-start.4 = (bf16[8,8,2048]{2,1,0:T(8,128)(2,1)S(1)}, bf16[8,8,2048]{2,1,0:T(8,128)(2,1)S(1)}, u32[]{:S(2)}, u32[]{:S(2)}) collective-permute-start(bf16[8,8,2048]{2,1,0:T(8,128)(2,1)S(1)} %all-to-all-done.receivers), channel_id=1, source_target_pairs={{1,0},{0,1},{3,2},{2,3},{5,4},{4,5},{7,6},{6,7},{9,8},{8,9},{11,10... | collective-permute-start | bytes 786440 | tf_op jit(solution)/shard_map/ppermute | solution.py:416

commit v4 on v3

--- a/solution.py
+++ b/solution.py
@@ -3,6 +3,7 @@
 
 import jax
 import jax.numpy as jnp
+import ml_dtypes
 import numpy as np
 from jax import lax
 from jax.experimental import pallas as pl
@@ -39,7 +40,7 @@
     matrix = np.zeros((6 * LANES, LANES))
     for n in range(LANES):
         matrix[DEC * n : DEC * n + TAPS, n] = taps
-    return matrix.astype(np.float32)
+    return np.concatenate(thirds(matrix), axis=1)
 
 
 def tile_bins():
@@ -59,29 +60,20 @@
     return bins, first
 
 
+def thirds(values):
+    parts = []
+    rest = values.astype(np.float64)
+    for _ in range(3):
+        parts.append(rest.astype(np.float32).astype(ml_dtypes.bfloat16))
+        rest = rest - parts[-1].astype(np.float64)
+    return parts
+
+
 def fourier_tiles():
-    bins, half_of = tile_bins()
-    m = np.arange(LANES)
-    tiles = np.zeros((8, 2 * LANES, 2 * LANES))
-    for tile in range(8):
-        for column in range(LANES):
-            f = bins[tile, column]
-            if f < 0:
-                continue
-            angle = 2.0 * np.pi * ((f * m) % NT) / NT
-            c, s = np.cos(angle), np.sin(angle)
-            half = half_of[tile, column]
-            if tile == 0:
-                rows = slice(half * LANES, (half + 1) * LANES)
-                tiles[tile, rows, column] = c
-                tiles[tile, rows, LANES + column] = -s
-            else:
-                sign = 1.0 if half == 0 else -1.0
-                tiles[tile, :LANES, column] = c
-                tiles[tile, LANES:, column] = sign * s
-                tiles[tile, :LANES, LANES + column] = -s
-                tiles[tile, LANES:, LANES + column] = sign * c
-    return tiles.astype(np.float32)
+    bins, _ = tile_bins()
+    angle = 2.0 * np.pi * ((bins[:, None, :] * np.arange(LANES)[None, :, None]) % NT) / NT
+    used = bins[:, None, :] >= 0
+    return np.stack(thirds(np.concatenate([used * np.cos(angle), used * np.sin(angle)], axis=2)))
 
 
 def band_bins():
@@ -153,6 +145,17 @@
     low = jnp.where(half == 0, tile, jnp.where(tile == 0, GROUP // 2, GROUP - tile))
     used = is_band | (within % 64 < 32)
     return jnp.where(used, GROUP * high + low, -1000).astype(jnp.float32)
+
+
+def split(values):
+    first = values.astype(jnp.bfloat16)
+    rest = values - first.astype(jnp.float32)
+    second = rest.astype(jnp.bfloat16)
+    return [first, second, (rest - second.astype(jnp.float32)).astype(jnp.bfloat16)]
+
+
+def product(left, right):
+    return jnp.dot(left, right, preferred_element_type=jnp.float32)
 
 
 def whiten_kernel(
@@ -193,22 +196,33 @@
             if part == 0 and run > 0:
                 raw[(run - 1) * 16 + w * 8 : (run - 1) * 16 + w * 8 + 8, 5 * LANES :] = moved
     copies[2].wait()
-    traces = jnp.dot(raw[...], decimate[...], precision=lax.Precision.HIGHEST, preferred_element_type=jnp.float32)
+    rows = raw.shape[0]
+    parts = split(raw[...])
+    wide = product(jnp.concatenate(parts, axis=0), decimate[:, : 2 * LANES])
+    traces = product(parts[0], decimate[:, 2 * LANES :])
+    traces = traces + wide[2 * rows :, :LANES] + wide[rows : 2 * rows, LANES:]
+    traces = traces + (wide[:rows, LANES:] + wide[rows : 2 * rows, :LANES]) + wide[:rows, :LANES]
     parts = small_fourier([(traces[16 * run : 16 * run + 16], None) for run in range(GROUP)])
-    left = lax.broadcasted_iota(jnp.int32, (16, LANES), 1) < 64
+    lane = lax.broadcasted_iota(jnp.int32, (16, LANES), 1)
+    left = lane < 64
     copies[3].wait()
     real_tiles, imag_tiles = [], []
     for tile in range(8):
+        pair = (parts[0][0], parts[8][0]) if tile == 0 else parts[tile]
+        pieces = split(jnp.concatenate(pair, axis=0))
+        both = product(jnp.concatenate(pieces, axis=0), fourier[0, tile])
+        middle = product(jnp.concatenate(pieces[:2], axis=0), fourier[1, tile])
+        low = product(pieces[0], fourier[2, tile])
+        both = low + both[64:] + middle[32:] + (both[32:64] + middle[:32]) + both[:32]
+        first_cos, first_sin = both[:16, :LANES], both[:16, LANES:]
+        second_cos, second_sin = both[16:, :LANES], both[16:, LANES:]
+        upper = jnp.where(lane // 64 == tile % 2, lane % 64 // 32, lane % 8 // 4) == 0
         if tile == 0:
-            pair = [parts[0][0], parts[8][0]]
+            real_tiles.append(jnp.where(upper, first_cos, second_cos))
+            imag_tiles.append(-jnp.where(upper, first_sin, second_sin))
         else:
-            pair = list(parts[tile])
-        both = jnp.dot(
-            jnp.concatenate(pair, axis=1), fourier[tile], precision=lax.Precision.HIGHEST,
-            preferred_element_type=jnp.float32,
-        )
-        real_tiles.append(both[:, :LANES])
-        imag_tiles.append(both[:, LANES:])
+            real_tiles.append(first_cos + jnp.where(upper, second_sin, -second_sin))
+            imag_tiles.append(jnp.where(upper, second_cos, -second_cos) - first_sin)
     reals, imags, powers = [], [], []
     extra = None
     for pair in range(4):
@@ -220,10 +234,6 @@
         powers.append(jnp.where(left, pa, pb))
         extra = plus(extra, jnp.where(left, pb, pa))
     power = jnp.concatenate(powers + [extra], axis=1)
-    first = power.astype(jnp.bfloat16)
-    rest = power - first.astype(jnp.float32)
-    second = rest.astype(jnp.bfloat16)
-    third = (rest - second.astype(jnp.float32)).astype(jnp.bfloat16)
     copies[4].wait()
     bins = source_bins()
     window = jnp.concatenate(
@@ -233,9 +243,7 @@
         ],
         axis=1,
     )
-    sums = jnp.dot(
-        jnp.concatenate([first, second, third], axis=0), window, preferred_element_type=jnp.float32
-    )
+    sums = product(jnp.concatenate(split(power), axis=0), window)
     smoothed = (sums[:16] + sums[16:32] + sums[32:]) * smooth[1:2, :]
     gain = lax.rsqrt(smoothed + EPS)
     for q, values in enumerate((reals, imags)):
@@ -263,8 +271,8 @@
         scratch_shapes=[
             pltpu.SMEM((WINDOWS,), jnp.int32),
             pltpu.VMEM(records.shape, jnp.float32),
-            pltpu.VMEM(decimate.shape, jnp.float32),
-            pltpu.VMEM(fourier.shape, jnp.float32),
+            pltpu.VMEM(decimate.shape, jnp.bfloat16),
+            pltpu.VMEM(fourier.shape, jnp.bfloat16),
             pltpu.VMEM(smooth.shape, jnp.float32),
             pltpu.VMEM((16 * GROUP, 6 * LANES), jnp.float32),
             pltpu.SemaphoreType.DMA((5,)),
@@ -332,44 +340,51 @@
 
     src, rcv = lax.axis_index("src"), lax.axis_index("rcv")
     y_hi = (rcv + flip) % 2
-    for piece in range(PER):
-        held = receivers[piece].astype(jnp.float32)
+    for couple in range(PER // 2):
+        held = []
+        for k in range(2):
+            block = 2 * (PER * step + 2 * couple + k) + y_hi
+            wanted = jnp.where((block >= rcv) & (mask[block] > 0), 1.0, 0.0)
+            held.append(receivers[2 * couple + k].astype(jnp.float32) * wanted)
+        held = jnp.concatenate(held, axis=0)
         for w in range(WINDOWS):
             at_w = 2 * w * FB
             real, imag = held[:, at_w : at_w + FB], held[:, at_w + FB : at_w + 2 * FB]
-            for pair in range(COARSE // 2):
-                reals, imags = [], []
-                for k in range(2):
-                    lag = 2 * pair + k
-                    c = jnp.broadcast_to(coarse[0, lag : lag + 1], (PIECE, FB))
-                    s = jnp.broadcast_to(coarse[1, lag : lag + 1], (PIECE, FB))
-                    reals.append(real * c - imag * s)
-                    imags.append(real * s + imag * c)
-                row = piece * COARSE * PIECE + pair * 16
-                spread[row : row + 16, at_w : at_w + FB] = jnp.concatenate(reals, 0).astype(jnp.bfloat16)
-                spread[row : row + 16, at_w + FB : at_w + 2 * FB] = jnp.concatenate(imags, 0).astype(jnp.bfloat16)
-
-    sublane = lax.broadcasted_iota(jnp.int32, (PIECE, LANES), 0)
-    limits = []
-    for piece in range(PER):
-        block = 2 * (PER * step + piece) + y_hi
-        limit = jnp.where(block == rcv, src * PIECE, 4096)
-        limits.append(sublane + jnp.where((block >= rcv) & (mask[block] > 0), limit, -4096))
+            for lag in range(COARSE):
+                c = jnp.broadcast_to(coarse[0, lag : lag + 1], (2 * PIECE, FB))
+                s = jnp.broadcast_to(coarse[1, lag : lag + 1], (2 * PIECE, FB))
+                row = (couple * COARSE + lag) * 2 * PIECE
+                spread[row : row + 16, at_w : at_w + FB] = (real * c - imag * s).astype(jnp.bfloat16)
+                spread[row : row + 16, at_w + FB : at_w + 2 * FB] = (real * s + imag * c).astype(jnp.bfloat16)
+
     for chunk in range(4):
         lagged = lax.dot_general(
             spread[...], turned[chunk * 256 : (chunk + 1) * 256, :], (((1,), (1,)), ((), ())),
             preferred_element_type=jnp.float32,
         )
-        for piece in range(PER):
+        for couple in range(PER // 2):
             for half in range(2):
-                rows = piece * COARSE * PIECE
+                rows = couple * COARSE * 2 * PIECE
                 values = [
-                    lagged[rows + lag * PIECE : rows + (lag + 1) * PIECE, half * LANES : (half + 1) * LANES]
+                    lagged[
+                        rows + lag * 2 * PIECE : rows + (lag + 1) * 2 * PIECE, half * LANES : (half + 1) * LANES
+                    ].astype(jnp.bfloat16)
                     for lag in range(COARSE)
                 ]
                 for k, value in enumerate(swap_groups(values)):
                     source = chunk * 32 + half * 16 + k
-                    out[source, piece, 0] = jnp.where(limits[piece] > source, value, 0.0).astype(jnp.bfloat16)
+                    out[source, 2 * couple : 2 * couple + 2] = value.reshape(2, PIECE, LAGS)
+
+    if not flip:
+        @pl.when(step == rcv // 2 // PER)
+        def _():
+            at = rcv // 2 % PER
+            receiver = src * PIECE + lax.broadcasted_iota(jnp.int32, (PIECE, LAGS), 0)
+
+            @pl.loop(0, 128)
+            def _(source):
+                kept = jnp.where(receiver > source, out[source, at].astype(jnp.float32), 0.0)
+                out[source, at] = kept.astype(jnp.bfloat16)
 
 
 def correlate(mask, receivers, flip, *rest):
@@ -387,7 +402,7 @@
     ]
     result = jax.ShapeDtypeStruct((128, 8, 2, PIECE, LAGS), jnp.bfloat16)
     turned = jax.ShapeDtypeStruct((128 * FINE, SPEC), jnp.bfloat16)
-    block = pl.BlockSpec((128, PER, 1, PIECE, LAGS), place)
+    block = pl.BlockSpec((128, PER, None, PIECE, LAGS), place)
     spread = pltpu.VMEM((PER * COARSE * PIECE, SPEC), jnp.bfloat16)
     common = dict(
         grid=(8 // PER,),

time: 50.8 us -> 49.4 us (0.972)
  Pallas kernels: 22.9 us -> 21.5 us
    pallas_call x1, Pallas kernels: 5.69 us -> 4.18 us  [whiten(): pl.pallas_call(whiten_kernel, out_shape=(jax.ShapeDtypeStruct((8, PIECE,...]
  transfers between devices with their start and end apart: 7 -> 7, of which waited for: 4 -> 4; matrix products, arithmetic and copies ran while one was open for 1% -> 2% of each run, Pallas kernels for 19% -> 20%
where the time goes in v4:
time: 49.4 us; the launch traced here: 49.2 us
  starting transfers between devices  21.6 us (44%)
  Pallas kernels  21.5 us (44%)
  waiting for transfers between devices  4.58 us (9%)
  other arithmetic  0.75 us (2%)
  between operations  0.67 us (1%)
    pallas_call x2, Pallas kernels, correlate(): pl.pallas_call(functools.partial(correlate_kernel, flip), in_specs=in_spe...  17.3 us
    ppermute x6, starting transfers between devices, move(): lax.ppermute(block, axis, [(source_of(i), i) for i in range(lax.axis_size...  12.6 us
    all_to_all x1, starting transfers between devices, on_device(): receivers = lax.all_to_all(copies, 'rcv', 0, 0, axis_index_groups=CHIPS)  9.03 us
    ppermute x6, waiting for transfers between devices, move(): lax.ppermute(block, axis, [(source_of(i), i) for i in range(lax.axis_size...  4.58 us
    pallas_call x1, Pallas kernels, whiten(): pl.pallas_call(whiten_kernel, out_shape=(jax.ShapeDtypeStruct((8, PIECE,...  4.18 us
  transfers between devices with their start and end apart: 7, of which 4 were waited for; matrix products, arithmetic and copies ran while one was open for 2% of the time, Pallas kernels for 20%

profile of v4, /device:TPU:1, one launch (start us, length us, event | category | flops | bytes accessed | tf_op | source)
XLA Modules:
  0.0 49.2 jit_solution(221444761619424073)
XLA Ops:
  0.0 0.0 copy-start.1
  0.0 0.0 copy-start.2
  0.0 0.0 copy-start
  0.0 4.2 %shard_map.91 = (bf16[8,8,2048]{2,1,0:T(8,128)(2,1)}, bf16[8,2048]{1,0:T(8,128)(2,1)S(1)}) custom-call(s32[2]{0:T(128)} %starts_hbm.1, f32[8,20480]{1,0:T(8,128)} %records_hbm.1, bf16[768,384]{1,0:T(8,128)(2,1)} %constant.45.clone.decimate_hbm, bf16[3,8,128,256]{3,2,1,0:T(8,128)(2,1)} %constant.46.clone.fourier_hbm, f32[2,512]{1,0:T(2,128)} %constant.47.clone.smooth_hbm), custom_call_target="tpu_custom_call" | custom-call | tf_op jit(solution)/shard_map/pallas_call | solution.py:263
  4.2 9.0 %all-to-all-start = ((bf16[8,8,2048]{2,1,0:T(8,128)(2,1)}), bf16[8,8,2048]{2,1,0:T(8,128)(2,1)S(1)}, u32[]{:S(2)}, u32[]{:S(2)}) async-start(bf16[8,8,2048]{2,1,0:T(8,128)(2,1)} %get-tuple-element.17), calls=%async_computation | async-start | bytes 524288 | tf_op jit(solution)/shard_map/all_to_all | solution.py:453
  13.2 1.3 %collective-permute-start.5 = (bf16[8,2048]{1,0:T(8,128)(2,1)S(1)}, bf16[8,2048]{1,0:T(8,128)(2,1)S(1)}, u32[]{:S(2)}, u32[]{:S(2)}) collective-permute-start(bf16[8,2048]{1,0:T(8,128)(2,1)S(1)} %get-tuple-element.18), channel_id=1, source_target_pairs={{32,0},{48,16},{0,32},{16,48},{96,64},{112,80},{64,96},{80,112},{1... | collective-permute-start | bytes 98312 | tf_op jit(solution)/shard_map/ppermute | solution.py:431
  15.2 0.8 %collective-permute-done.5 = bf16[8,2048]{1,0:T(8,128)(2,1)S(1)} collective-permute-done((bf16[8,2048]{1,0:T(8,128)(2,1)S(1)}, bf16[8,2048]{1,0:T(8,128)(2,1)S(1)}, u32[]{:S(2)}, u32[]{:S(2)}) %collective-permute-start.5) | collective-permute-done | bytes 32800 | tf_op jit(solution)/shard_map/ppermute | solution.py:431
  16.0 12.9 %conditional.1 = (bf16[8,8,2048]{2,1,0:T(8,128)(2,1)}, bf16[8,8,2048]{2,1,0:T(8,128)(2,1)}) conditional(s32[]{:T(128)} %bitcast.3, () %tuple.13, (bf16[8,2048]{1,0:T(8,128)(2,1)S(1)}, bf16[8,2048]{1,0:T(8,128)(2,1)S(1)}) %tuple.14), branch_computations={%region_0.0_spmd, %region_1.2_spmd} | conditional | flops 491550 | bytes 2490845 | solution.py:454
  16.0 1.3 %collective-permute-start.2 = (bf16[2,8,2048]{2,1,0:T(8,128)(2,1)S(1)}, bf16[2,8,2048]{2,1,0:T(8,128)(2,1)S(1)}, u32[]{:S(2)}, u32[]{:S(2)}) collective-permute-start(bf16[2,8,2048]{2,1,0:T(8,128)(2,1)S(1)} %maximum_select_fusion), channel_id=1, source_target_pairs={{192,0},{208,16},{224,32},{240,48},{0,64},{16,80},{32,96},{48,112}... | collective-permute-start | bytes 196616 | tf_op jit(solution)/shard_map/cond/branch_1_fun/ppermute | solution.py:431
  17.3 2.4 %collective-permute-start.1 = (bf16[2,8,2048]{2,1,0:T(8,128)(2,1)S(1)}, bf16[2,8,2048]{2,1,0:T(8,128)(2,1)S(1)}, u32[]{:S(2)}, u32[]{:S(2)}) collective-permute-start(bf16[2,8,2048]{2,1,0:T(8,128)(2,1)S(1)} %maximum_select_fusion), channel_id=1, source_target_pairs={{128,0},{144,16},{160,32},{176,48},{192,64},{208,80},{224,96},{240... | collective-permute-start | bytes 196616 | tf_op jit(solution)/shard_map/cond/branch_1_fun/ppermute | solution.py:431
  19.7 1.2 %collective-permute-start = (bf16[2,8,2048]{2,1,0:T(8,128)(2,1)S(1)}, bf16[2,8,2048]{2,1,0:T(8,128)(2,1)S(1)}, u32[]{:S(2)}, u32[]{:S(2)}) collective-permute-start(bf16[2,8,2048]{2,1,0:T(8,128)(2,1)S(1)} %maximum_select_fusion), channel_id=1, source_target_pairs={{64,0},{80,16},{96,32},{112,48},{128,64},{144,80},{160,96},{176,11... | collective-permute-start | bytes 196616 | tf_op jit(solution)/shard_map/cond/branch_1_fun/ppermute | solution.py:431
  20.9 0.0 collective-permute-done.2
  20.9 1.2 %collective-permute-done.1 = bf16[2,8,2048]{2,1,0:T(8,128)(2,1)S(1)} collective-permute-done((bf16[2,8,2048]{2,1,0:T(8,128)(2,1)S(1)}, bf16[2,8,2048]{2,1,0:T(8,128)(2,1)S(1)}, u32[]{:S(2)}, u32[]{:S(2)}) %collective-permute-start.1) | collective-permute-done | bytes 65568 | tf_op jit(solution)/shard_map/cond/branch_1_fun/ppermute | solution.py:431
  22.1 1.1 %collective-permute-done = bf16[2,8,2048]{2,1,0:T(8,128)(2,1)S(1)} collective-permute-done((bf16[2,8,2048]{2,1,0:T(8,128)(2,1)S(1)}, bf16[2,8,2048]{2,1,0:T(8,128)(2,1)S(1)}, u32[]{:S(2)}, u32[]{:S(2)}) %collective-permute-start) | collective-permute-done | bytes 65568 | tf_op jit(solution)/shard_map/cond/branch_1_fun/ppermute | solution.py:431
  23.2 0.7 %pad_maximum_fusion = bf16[8,8,2048]{2,1,0:T(8,128)(2,1)} fusion(bf16[2,8,2048]{2,1,0:T(8,128)(2,1)S(1)} %collective-permute-done.2, bf16[2,8,2048]{2,1,0:T(8,128)(2,1)S(1)} %collective-permute-done.1, bf16[2,8,2048]{2,1,0:T(8,128)(2,1)S(1)} %collective-permute-done, bf16[2,8,2048]{2,1,0:T(8,128)(2,1)S(1)} %maximum_select_fusion), kind=kLoop, calls=%fused_computation | loop fusion | flops 393216 | bytes 524288 | tf_op jit(solution)/shard_map/cond/branch_1_fun/concatenate | solution.py:440
  23.9 3.5 %collective-permute-start.3 = (bf16[8,8,2048]{2,1,0:T(8,128)(2,1)}, bf16[8,8,2048]{2,1,0:T(8,128)(2,1)}, u32[]{:S(2)}, u32[]{:S(2)}) collective-permute-start(bf16[8,8,2048]{2,1,0:T(8,128)(2,1)} %pad_maximum_fusion), channel_id=1, source_target_pairs={{16,0},{0,16},{48,32},{32,48},{80,64},{64,80},{112,96},{96,112},{1... | collective-permute-start | bytes 786440 | tf_op jit(solution)/shard_map/cond/branch_1_fun/ppermute | solution.py:431
  27.4 1.5 %collective-permute-done.3 = bf16[8,8,2048]{2,1,0:T(8,128)(2,1)} collective-permute-done((bf16[8,8,2048]{2,1,0:T(8,128)(2,1)}, bf16[8,8,2048]{2,1,0:T(8,128)(2,1)}, u32[]{:S(2)}, u32[]{:S(2)}) %collective-permute-start.3) | collective-permute-done | bytes 262176 | tf_op jit(solution)/shard_map/cond/branch_1_fun/ppermute | solution.py:431
  28.9 0.0 all-to-all-done.receivers
  28.9 2.9 %collective-permute-start.4 = (bf16[8,8,2048]{2,1,0:T(8,128)(2,1)S(1)}, bf16[8,8,2048]{2,1,0:T(8,128)(2,1)S(1)}, u32[]{:S(2)}, u32[]{:S(2)}) collective-permute-start(bf16[8,8,2048]{2,1,0:T(8,128)(2,1)S(1)} %all-to-all-done.receivers), channel_id=1, source_target_pairs={{1,0},{0,1},{3,2},{2,3},{5,4},{4,5},{7,6},{6,7},{9,8},{8,9},{11,10... | collective-permute-start | bytes 786440 | tf_op jit(solution)/shard_map/ppermute | solution.py:431
  31.8 0.0 copy-done.1
  31.8 0.0 copy-done.2
  31.8 0.0 copy-done
  31.8 9.9 %shard_map.92 = (bf16[128,8,2,8,128]{4,3,2,1,0:T(8,128)(2,1)}, bf16[1024,2048]{1,0:T(8,128)(2,1)S(1)}) custom-call(s32[16]{0:T(128)S(1)} %bitcast.8, bf16[8,8,2048]{2,1,0:T(8,128)(2,1)S(1)} %all-to-all-done.receivers, f32[2,16,512]{2,1,0:T(8,128)S(1)} %copy-done.1, bf16[8,8,2048]{2,1,0:T(8,128)(2,1)} %get-tuple-element.19.rest_0_, ...), custom_call_target="tpu_custom_call" | custom-call | flops 4294967296 | bytes 6291456 | tf_op jit(solution)/shard_map/pallas_call | solution.py:422
  41.7 0.0 collective-permute-done.4.receivers
  41.8 7.4 %shard_map.93 = bf16[128,8,2,8,128]{4,3,2,1,0:T(8,128)(2,1)} custom-call(s32[16]{0:T(128)S(1)} %bitcast.9, bf16[8,8,2048]{2,1,0:T(8,128)(2,1)S(1)} %collective-permute-done.4.receivers, f32[2,16,512]{2,1,0:T(8,128)S(1)} %copy-done.1, bf16[1024,2048]{1,0:T(8,128)(2,1)S(1)} %get-tuple-element.21.rest_0_, ...), custom_call_target="tpu_custom_call", output_to_operand_aliasing={{}: (4, {})} | custom-call | flops 4294967296 | bytes 6291456 | tf_op jit(solution)/shard_map/pallas_call | solution.py:416
  (1 shorter events, 0.0 us)
Async XLA Ops:
  0.0 31.8 %copy-start.1 = (f32[2,16,512]{2,1,0:T(8,128)S(1)}, f32[2,16,512]{2,1,0:T(8,128)}, u32[]{:S(2)}) copy-start(f32[2,16,512]{2,1,0:T(8,128)} %constant.48.clone.coarse) | copy-start | bytes 196612
  0.0 31.8 %copy-start.2 = (f32[2,8,512]{2,1,0:T(8,128)S(1)}, f32[2,8,512]{2,1,0:T(8,128)}, u32[]{:S(2)}) copy-start(f32[2,8,512]{2,1,0:T(8,128)} %constant.49.clone.rest_2_) | copy-start | bytes 98308
  0.0 31.8 %copy-start = (s32[1,16,1]{1,2,0:T(1,128)S(1)}, s32[1,16,1]{1,2,0:T(1,128)}, u32[]{:S(2)}) copy-start(s32[1,16,1]{1,2,0:T(1,128)} %param.13) | copy-start | bytes 196
  4.2 24.7 %all-to-all-start = ((bf16[8,8,2048]{2,1,0:T(8,128)(2,1)}), bf16[8,8,2048]{2,1,0:T(8,128)(2,1)S(1)}, u32[]{:S(2)}, u32[]{:S(2)}) async-start(bf16[8,8,2048]{2,1,0:T(8,128)(2,1)} %get-tuple-element.17), calls=%async_computation | async-start | bytes 524288 | tf_op jit(solution)/shard_map/all_to_all | solution.py:453
  13.2 2.8 %collective-permute-start.5 = (bf16[8,2048]{1,0:T(8,128)(2,1)S(1)}, bf16[8,2048]{1,0:T(8,128)(2,1)S(1)}, u32[]{:S(2)}, u32[]{:S(2)}) collective-permute-start(bf16[8,2048]{1,0:T(8,128)(2,1)S(1)} %get-tuple-element.18), channel_id=1, source_target_pairs={{32,0},{48,16},{0,32},{16,48},{96,64},{112,80},{64,96},{80,112},{1... | collective-permute-start | bytes 98312 | tf_op jit(solution)/shard_map/ppermute | solution.py:431
  16.0 4.9 %collective-permute-start.2 = (bf16[2,8,2048]{2,1,0:T(8,128)(2,1)S(1)}, bf16[2,8,2048]{2,1,0:T(8,128)(2,1)S(1)}, u32[]{:S(2)}, u32[]{:S(2)}) collective-permute-start(bf16[2,8,2048]{2,1,0:T(8,128)(2,1)S(1)} %maximum_select_fusion), channel_id=1, source_target_pairs={{192,0},{208,16},{224,32},{240,48},{0,64},{16,80},{32,96},{48,112}... | collective-permute-start | bytes 196616 | tf_op jit(solution)/shard_map/cond/branch_1_fun/ppermute | solution.py:431
  17.3 4.8 %collective-permute-start.1 = (bf16[2,8,2048]{2,1,0:T(8,128)(2,1)S(1)}, bf16[2,8,2048]{2,1,0:T(8,128)(2,1)S(1)}, u32[]{:S(2)}, u32[]{:S(2)}) collective-permute-start(bf16[2,8,2048]{2,1,0:T(8,128)(2,1)S(1)} %maximum_select_fusion), channel_id=1, source_target_pairs={{128,0},{144,16},{160,32},{176,48},{192,64},{208,80},{224,96},{240... | collective-permute-start | bytes 196616 | tf_op jit(solution)/shard_map/cond/branch_1_fun/ppermute | solution.py:431
  19.7 3.4 %collective-permute-start = (bf16[2,8,2048]{2,1,0:T(8,128)(2,1)S(1)}, bf16[2,8,2048]{2,1,0:T(8,128)(2,1)S(1)}, u32[]{:S(2)}, u32[]{:S(2)}) collective-permute-start(bf16[2,8,2048]{2,1,0:T(8,128)(2,1)S(1)} %maximum_select_fusion), channel_id=1, source_target_pairs={{64,0},{80,16},{96,32},{112,48},{128,64},{144,80},{160,96},{176,11... | collective-permute-start | bytes 196616 | tf_op jit(solution)/shard_map/cond/branch_1_fun/ppermute | solution.py:431
  23.9 5.0 %collective-permute-start.3 = (bf16[8,8,2048]{2,1,0:T(8,128)(2,1)}, bf16[8,8,2048]{2,1,0:T(8,128)(2,1)}, u32[]{:S(2)}, u32[]{:S(2)}) collective-permute-start(bf16[8,8,2048]{2,1,0:T(8,128)(2,1)} %pad_maximum_fusion), channel_id=1, source_target_pairs={{16,0},{0,16},{48,32},{32,48},{80,64},{64,80},{112,96},{96,112},{1... | collective-permute-start | bytes 786440 | tf_op jit(solution)/shard_map/cond/branch_1_fun/ppermute | solution.py:431
  28.9 12.8 %collective-permute-start.4 = (bf16[8,8,2048]{2,1,0:T(8,128)(2,1)S(1)}, bf16[8,8,2048]{2,1,0:T(8,128)(2,1)S(1)}, u32[]{:S(2)}, u32[]{:S(2)}) collective-permute-start(bf16[8,8,2048]{2,1,0:T(8,128)(2,1)S(1)} %all-to-all-done.receivers), channel_id=1, source_target_pairs={{1,0},{0,1},{3,2},{2,3},{5,4},{4,5},{7,6},{6,7},{9,8},{8,9},{11,10... | collective-permute-start | bytes 786440 | tf_op jit(solution)/shard_map/ppermute | solution.py:431

commit v5 on v4

--- a/solution.py
+++ b/solution.py
@@ -340,12 +340,16 @@
 
     src, rcv = lax.axis_index("src"), lax.axis_index("rcv")
     y_hi = (rcv + flip) % 2
+    limits = []
     for couple in range(PER // 2):
-        held = []
+        held, limit = [], []
         for k in range(2):
             block = 2 * (PER * step + 2 * couple + k) + y_hi
             wanted = jnp.where((block >= rcv) & (mask[block] > 0), 1.0, 0.0)
             held.append(receivers[2 * couple + k].astype(jnp.float32) * wanted)
+            channel = lax.broadcasted_iota(jnp.int32, (PIECE, LANES), 0) + src * PIECE
+            limit.append(jnp.where(block == rcv, channel, 4096).astype(jnp.float32))
+        limits.append(jnp.concatenate(limit, axis=0).astype(jnp.bfloat16))
         held = jnp.concatenate(held, axis=0)
         for w in range(WINDOWS):
             at_w = 2 * w * FB
@@ -373,18 +377,9 @@
                 ]
                 for k, value in enumerate(swap_groups(values)):
                     source = chunk * 32 + half * 16 + k
+                    if not flip:
+                        value = value * jnp.clip(limits[couple] - source, 0, 1)
                     out[source, 2 * couple : 2 * couple + 2] = value.reshape(2, PIECE, LAGS)
-
-    if not flip:
-        @pl.when(step == rcv // 2 // PER)
-        def _():
-            at = rcv // 2 % PER
-            receiver = src * PIECE + lax.broadcasted_iota(jnp.int32, (PIECE, LAGS), 0)
-
-            @pl.loop(0, 128)
-            def _(source):
-                kept = jnp.where(receiver > source, out[source, at].astype(jnp.float32), 0.0)
-                out[source, at] = kept.astype(jnp.bfloat16)
 
 
 def correlate(mask, receivers, flip, *rest):
@@ -437,21 +432,21 @@
 def gather_sources(own, near):
     y_lo = lax.axis_index("src") // 2 % 2
     two = jnp.where(y_lo == 0, jnp.stack([own, near]), jnp.stack([near, own]))
-    mine = jnp.concatenate([two] + [
+    return jnp.concatenate([two] + [
         move(two, "src", lambda i, k=k: ((i // 4 + k) % 4) * 4 + i % 4) for k in (1, 2, 3)
     ])
-    return mine, move(mine, "src", lambda i: i ^ 1)
 
 
 def no_sources(own, near):
-    return (jnp.zeros((8, PIECE, SPEC), own.dtype),) * 2
+    return jnp.zeros((8, PIECE, SPEC), own.dtype)
 
 
 def on_device(records, starts, block_mask):
     copies, own = whiten(records, starts)
     near = move(own, "src", lambda i: i ^ 2)
     receivers = lax.all_to_all(copies, "rcv", 0, 0, axis_index_groups=CHIPS)
-    mine, other = lax.cond(starts[0] >= 0, gather_sources, no_sources, own, near)
+    mine = lax.cond(starts[0] >= 0, gather_sources, no_sources, own, near)
+    other = move(mine, "src", lambda i: i ^ 1)
     far = move(receivers, "rcv", lambda i: i ^ 1)
     mask = block_mask.reshape(-1)
     result, turned = correlate(mask, receivers, 0, mine, other)

time: 49.4 us -> 46.1 us (0.933)
  waiting for transfers between devices: 4.58 us -> 3.08 us
  Pallas kernels: 21.5 us -> 20.3 us
  other arithmetic: 0.75 us -> 0.04 us
    ppermute x6, waiting for transfers between devices: 4.58 us -> 3.08 us  [move(): lax.ppermute(block, axis, [(source_of(i), i) for i in range(lax.axis_size...]
    pallas_call x2, Pallas kernels: 17.3 us -> 16.1 us  [correlate(): pl.pallas_call(functools.partial(correlate_kernel, flip), in_specs=in_spe...]
    concatenate x1, other arithmetic: 0.74 us -> 0.04 us  [gather_sources(): jnp.concatenate([two] + [move(two, 'src', lambda i, k=k: (i // 4 + k) % 4...]
  transfers between devices with their start and end apart: 7 -> 7, of which waited for: 4 -> 3; matrix products, arithmetic and copies ran while one was open for 2% -> 0% of each run, Pallas kernels for 20% -> 19%
where the time goes in v5:
time: 46.1 us; the launch traced here: 45.9 us
  starting transfers between devices  21.8 us (47%)
  Pallas kernels  20.3 us (44%)
  waiting for transfers between devices  3.08 us (7%)
  between operations  0.69 us (1%)
    pallas_call x2, Pallas kernels, correlate(): pl.pallas_call(functools.partial(correlate_kernel, flip), in_specs=in_spe...  16.1 us
    ppermute x6, starting transfers between devices, move(): lax.ppermute(block, axis, [(source_of(i), i) for i in range(lax.axis_size...  12.7 us
    all_to_all x1, starting transfers between devices, on_device(): receivers = lax.all_to_all(copies, 'rcv', 0, 0, axis_index_groups=CHIPS)  9.03 us
    pallas_call x1, Pallas kernels, whiten(): pl.pallas_call(whiten_kernel, out_shape=(jax.ShapeDtypeStruct((8, PIECE,...  4.18 us
    ppermute x6, waiting for transfers between devices, move(): lax.ppermute(block, axis, [(source_of(i), i) for i in range(lax.axis_size...  3.08 us
  transfers between devices with their start and end apart: 7, of which 3 were waited for; matrix products, arithmetic and copies ran while one was open for 0% of the time, Pallas kernels for 19%

profile of v5, /device:TPU:1, one launch (start us, length us, event | category | flops | bytes accessed | tf_op | source)
XLA Modules:
  0.0 45.9 jit_solution(9989453882185176632)
XLA Ops:
  0.0 0.0 copy-start.1
  0.0 0.0 copy-start.2
  0.0 0.0 copy-start
  0.0 4.2 %shard_map.91 = (bf16[8,8,2048]{2,1,0:T(8,128)(2,1)}, bf16[8,2048]{1,0:T(8,128)(2,1)S(1)}) custom-call(s32[2]{0:T(128)} %starts_hbm.1, f32[8,20480]{1,0:T(8,128)} %records_hbm.1, bf16[768,384]{1,0:T(8,128)(2,1)} %constant.45.clone.decimate_hbm, bf16[3,8,128,256]{3,2,1,0:T(8,128)(2,1)} %constant.46.clone.fourier_hbm, f32[2,512]{1,0:T(2,128)} %constant.47.clone.smooth_hbm), custom_call_target="tpu_custom_call" | custom-call | tf_op jit(solution)/shard_map/pallas_call | solution.py:263
  4.2 9.0 %all-to-all-start = ((bf16[8,8,2048]{2,1,0:T(8,128)(2,1)}), bf16[8,8,2048]{2,1,0:T(8,128)(2,1)S(1)}, u32[]{:S(2)}, u32[]{:S(2)}) async-start(bf16[8,8,2048]{2,1,0:T(8,128)(2,1)} %get-tuple-element.18), calls=%async_computation | async-start | bytes 524288 | tf_op jit(solution)/shard_map/all_to_all | solution.py:447
  13.2 1.3 %collective-permute-start.4 = (bf16[8,2048]{1,0:T(8,128)(2,1)S(1)}, bf16[8,2048]{1,0:T(8,128)(2,1)S(1)}, u32[]{:S(2)}, u32[]{:S(2)}) collective-permute-start(bf16[8,2048]{1,0:T(8,128)(2,1)S(1)} %get-tuple-element.19), channel_id=1, source_target_pairs={{32,0},{48,16},{0,32},{16,48},{96,64},{112,80},{64,96},{80,112},{1... | collective-permute-start | bytes 98312 | tf_op jit(solution)/shard_map/ppermute | solution.py:426
  15.2 0.8 %collective-permute-done.4 = bf16[8,2048]{1,0:T(8,128)(2,1)S(1)} collective-permute-done((bf16[8,2048]{1,0:T(8,128)(2,1)S(1)}, bf16[8,2048]{1,0:T(8,128)(2,1)S(1)}, u32[]{:S(2)}, u32[]{:S(2)}) %collective-permute-start.4) | collective-permute-done | bytes 32800 | tf_op jit(solution)/shard_map/ppermute | solution.py:426
  16.0 7.2 %conditional.1 = (bf16[8,8,2048]{2,1,0:T(8,128)(2,1)S(1)}) conditional(s32[]{:T(128)} %bitcast.3, () %tuple.11, (bf16[8,2048]{1,0:T(8,128)(2,1)S(1)}, bf16[8,2048]{1,0:T(8,128)(2,1)S(1)}) %tuple.12), branch_computations={%region_0.0_spmd, %region_1.2_spmd} | conditional | flops 491550 | bytes 1442221 | solution.py:448
  16.0 1.3 %collective-permute-start.2 = (bf16[2,8,2048]{2,1,0:T(8,128)(2,1)S(1)}, bf16[2,8,2048]{2,1,0:T(8,128)(2,1)S(1)}, u32[]{:S(2)}, u32[]{:S(2)}) collective-permute-start(bf16[2,8,2048]{2,1,0:T(8,128)(2,1)S(1)} %maximum_select_fusion), channel_id=1, source_target_pairs={{192,0},{208,16},{224,32},{240,48},{0,64},{16,80},{32,96},{48,112}... | collective-permute-start | bytes 196616 | tf_op jit(solution)/shard_map/cond/branch_1_fun/ppermute | solution.py:426
  17.3 2.4 %collective-permute-start.1 = (bf16[2,8,2048]{2,1,0:T(8,128)(2,1)S(1)}, bf16[2,8,2048]{2,1,0:T(8,128)(2,1)S(1)}, u32[]{:S(2)}, u32[]{:S(2)}) collective-permute-start(bf16[2,8,2048]{2,1,0:T(8,128)(2,1)S(1)} %maximum_select_fusion), channel_id=1, source_target_pairs={{128,0},{144,16},{160,32},{176,48},{192,64},{208,80},{224,96},{240... | collective-permute-start | bytes 196616 | tf_op jit(solution)/shard_map/cond/branch_1_fun/ppermute | solution.py:426
  19.7 1.2 %collective-permute-start = (bf16[2,8,2048]{2,1,0:T(8,128)(2,1)S(1)}, bf16[2,8,2048]{2,1,0:T(8,128)(2,1)S(1)}, u32[]{:S(2)}, u32[]{:S(2)}) collective-permute-start(bf16[2,8,2048]{2,1,0:T(8,128)(2,1)S(1)} %maximum_select_fusion), channel_id=1, source_target_pairs={{64,0},{80,16},{96,32},{112,48},{128,64},{144,80},{160,96},{176,11... | collective-permute-start | bytes 196616 | tf_op jit(solution)/shard_map/cond/branch_1_fun/ppermute | solution.py:426
  20.9 0.0 collective-permute-done.2
  20.9 1.2 %collective-permute-done.1 = bf16[2,8,2048]{2,1,0:T(8,128)(2,1)S(1)} collective-permute-done((bf16[2,8,2048]{2,1,0:T(8,128)(2,1)S(1)}, bf16[2,8,2048]{2,1,0:T(8,128)(2,1)S(1)}, u32[]{:S(2)}, u32[]{:S(2)}) %collective-permute-start.1) | collective-permute-done | bytes 65568 | tf_op jit(solution)/shard_map/cond/branch_1_fun/ppermute | solution.py:426
  22.1 1.1 %collective-permute-done = bf16[2,8,2048]{2,1,0:T(8,128)(2,1)S(1)} collective-permute-done((bf16[2,8,2048]{2,1,0:T(8,128)(2,1)S(1)}, bf16[2,8,2048]{2,1,0:T(8,128)(2,1)S(1)}, u32[]{:S(2)}, u32[]{:S(2)}) %collective-permute-start) | collective-permute-done | bytes 65568 | tf_op jit(solution)/shard_map/cond/branch_1_fun/ppermute | solution.py:426
  23.2 3.6 %collective-permute-start.5 = (bf16[8,8,2048]{2,1,0:T(8,128)(2,1)S(1)}, bf16[8,8,2048]{2,1,0:T(8,128)(2,1)S(1)}, u32[]{:S(2)}, u32[]{:S(2)}) collective-permute-start(bf16[8,8,2048]{2,1,0:T(8,128)(2,1)S(1)} %get-tuple-element.22.rest_0_), channel_id=1, source_target_pairs={{16,0},{0,16},{48,32},{32,48},{80,64},{64,80},{112,96},{96,112},{1... | collective-permute-start | bytes 786440 | tf_op jit(solution)/shard_map/ppermute | solution.py:426
  26.8 0.0 all-to-all-done.receivers
  26.8 2.9 %collective-permute-start.3 = (bf16[8,8,2048]{2,1,0:T(8,128)(2,1)S(1)}, bf16[8,8,2048]{2,1,0:T(8,128)(2,1)S(1)}, u32[]{:S(2)}, u32[]{:S(2)}) collective-permute-start(bf16[8,8,2048]{2,1,0:T(8,128)(2,1)S(1)} %all-to-all-done.receivers), channel_id=1, source_target_pairs={{1,0},{0,1},{3,2},{2,3},{5,4},{4,5},{7,6},{6,7},{9,8},{8,9},{11,10... | collective-permute-start | bytes 786440 | tf_op jit(solution)/shard_map/ppermute | solution.py:426
  29.7 0.0 collective-permute-done.5.rest_1_
  29.7 0.0 copy-done.1
  29.7 0.0 copy-done.2
  29.8 0.0 copy-done
  29.8 8.7 %shard_map.92 = (bf16[128,8,2,8,128]{4,3,2,1,0:T(8,128)(2,1)}, bf16[1024,2048]{1,0:T(8,128)(2,1)S(1)}) custom-call(s32[16]{0:T(128)S(1)} %bitcast.8, bf16[8,8,2048]{2,1,0:T(8,128)(2,1)S(1)} %all-to-all-done.receivers, f32[2,16,512]{2,1,0:T(8,128)S(1)} %copy-done.1, bf16[8,8,2048]{2,1,0:T(8,128)(2,1)S(1)} %get-tuple-element.22.rest_0_, ...), custom_call_target="tpu_custom_call" | custom-call | flops 4294967296 | bytes 6291456 | tf_op jit(solution)/shard_map/pallas_call | solution.py:417
  38.5 0.0 collective-permute-done.3.receivers
  38.5 7.4 %shard_map.93 = bf16[128,8,2,8,128]{4,3,2,1,0:T(8,128)(2,1)} custom-call(s32[16]{0:T(128)S(1)} %bitcast.9, bf16[8,8,2048]{2,1,0:T(8,128)(2,1)S(1)} %collective-permute-done.3.receivers, f32[2,16,512]{2,1,0:T(8,128)S(1)} %copy-done.1, bf16[1024,2048]{1,0:T(8,128)(2,1)S(1)} %get-tuple-element.20.rest_0_, ...), custom_call_target="tpu_custom_call", output_to_operand_aliasing={{}: (4, {})} | custom-call | flops 4294967296 | bytes 6291456 | tf_op jit(solution)/shard_map/pallas_call | solution.py:411
  (2 shorter events, 0.0 us)
Async XLA Ops:
  0.0 29.7 %copy-start.1 = (f32[2,16,512]{2,1,0:T(8,128)S(1)}, f32[2,16,512]{2,1,0:T(8,128)}, u32[]{:S(2)}) copy-start(f32[2,16,512]{2,1,0:T(8,128)} %constant.48.clone.coarse) | copy-start | bytes 196612
  0.0 29.7 %copy-start.2 = (f32[2,8,512]{2,1,0:T(8,128)S(1)}, f32[2,8,512]{2,1,0:T(8,128)}, u32[]{:S(2)}) copy-start(f32[2,8,512]{2,1,0:T(8,128)} %constant.49.clone.rest_2_) | copy-start | bytes 98308
  0.0 29.8 %copy-start = (s32[1,16,1]{1,2,0:T(1,128)S(1)}, s32[1,16,1]{1,2,0:T(1,128)}, u32[]{:S(2)}) copy-start(s32[1,16,1]{1,2,0:T(1,128)} %param.13) | copy-start | bytes 196
  4.2 22.6 %all-to-all-start = ((bf16[8,8,2048]{2,1,0:T(8,128)(2,1)}), bf16[8,8,2048]{2,1,0:T(8,128)(2,1)S(1)}, u32[]{:S(2)}, u32[]{:S(2)}) async-start(bf16[8,8,2048]{2,1,0:T(8,128)(2,1)} %get-tuple-element.18), calls=%async_computation | async-start | bytes 524288 | tf_op jit(solution)/shard_map/all_to_all | solution.py:447
  13.2 2.8 %collective-permute-start.4 = (bf16[8,2048]{1,0:T(8,128)(2,1)S(1)}, bf16[8,2048]{1,0:T(8,128)(2,1)S(1)}, u32[]{:S(2)}, u32[]{:S(2)}) collective-permute-start(bf16[8,2048]{1,0:T(8,128)(2,1)S(1)} %get-tuple-element.19), channel_id=1, source_target_pairs={{32,0},{48,16},{0,32},{16,48},{96,64},{112,80},{64,96},{80,112},{1... | collective-permute-start | bytes 98312 | tf_op jit(solution)/shard_map/ppermute | solution.py:426
  16.0 4.9 %collective-permute-start.2 = (bf16[2,8,2048]{2,1,0:T(8,128)(2,1)S(1)}, bf16[2,8,2048]{2,1,0:T(8,128)(2,1)S(1)}, u32[]{:S(2)}, u32[]{:S(2)}) collective-permute-start(bf16[2,8,2048]{2,1,0:T(8,128)(2,1)S(1)} %maximum_select_fusion), channel_id=1, source_target_pairs={{192,0},{208,16},{224,32},{240,48},{0,64},{16,80},{32,96},{48,112}... | collective-permute-start | bytes 196616 | tf_op jit(solution)/shard_map/cond/branch_1_fun/ppermute | solution.py:426
  17.3 4.8 %collective-permute-start.1 = (bf16[2,8,2048]{2,1,0:T(8,128)(2,1)S(1)}, bf16[2,8,2048]{2,1,0:T(8,128)(2,1)S(1)}, u32[]{:S(2)}, u32[]{:S(2)}) collective-permute-start(bf16[2,8,2048]{2,1,0:T(8,128)(2,1)S(1)} %maximum_select_fusion), channel_id=1, source_target_pairs={{128,0},{144,16},{160,32},{176,48},{192,64},{208,80},{224,96},{240... | collective-permute-start | bytes 196616 | tf_op jit(solution)/shard_map/cond/branch_1_fun/ppermute | solution.py:426
  19.7 3.4 %collective-permute-start = (bf16[2,8,2048]{2,1,0:T(8,128)(2,1)S(1)}, bf16[2,8,2048]{2,1,0:T(8,128)(2,1)S(1)}, u32[]{:S(2)}, u32[]{:S(2)}) collective-permute-start(bf16[2,8,2048]{2,1,0:T(8,128)(2,1)S(1)} %maximum_select_fusion), channel_id=1, source_target_pairs={{64,0},{80,16},{96,32},{112,48},{128,64},{144,80},{160,96},{176,11... | collective-permute-start | bytes 196616 | tf_op jit(solution)/shard_map/cond/branch_1_fun/ppermute | solution.py:426
  23.2 6.6 %collective-permute-start.5 = (bf16[8,8,2048]{2,1,0:T(8,128)(2,1)S(1)}, bf16[8,8,2048]{2,1,0:T(8,128)(2,1)S(1)}, u32[]{:S(2)}, u32[]{:S(2)}) collective-permute-start(bf16[8,8,2048]{2,1,0:T(8,128)(2,1)S(1)} %get-tuple-element.22.rest_0_), channel_id=1, source_target_pairs={{16,0},{0,16},{48,32},{32,48},{80,64},{64,80},{112,96},{96,112},{1... | collective-permute-start | bytes 786440 | tf_op jit(solution)/shard_map/ppermute | solution.py:426
  26.8 11.7 %collective-permute-start.3 = (bf16[8,8,2048]{2,1,0:T(8,128)(2,1)S(1)}, bf16[8,8,2048]{2,1,0:T(8,128)(2,1)S(1)}, u32[]{:S(2)}, u32[]{:S(2)}) collective-permute-start(bf16[8,8,2048]{2,1,0:T(8,128)(2,1)S(1)} %all-to-all-done.receivers), channel_id=1, source_target_pairs={{1,0},{0,1},{3,2},{2,3},{5,4},{4,5},{7,6},{6,7},{9,8},{8,9},{11,10... | collective-permute-start | bytes 786440 | tf_op jit(solution)/shard_map/ppermute | solution.py:426
